TPU v7x, 32 devices: a whole 2x2x4 slice. The times are simulated.
32 devices in a mesh: replica: 8 (over z, x), shard: 4 (over y, core).
Axes of the slice: x: 2, y: 2, z: 4, core: 2. Of those that a mesh axis runs over, the one named last changes fastest.
Arguments:
- tokens: bfloat16 [32, 1024, 768], P(('replica', 'shard')), may hold values from -6 to 6
- segments: int32 [32, 1024], P(('replica', 'shard')), may hold values from 0 to 3, never falling along the last dimension, each value on 1 to 512 neighbouring positions
- out_grad: bfloat16 [32, 1024, 768], P(('replica', 'shard')), may hold values from -6 to 6
- ln1_gain: bfloat16 [768], P('shard'), may hold values from 0.5 to 1.5
- ln1_bias: bfloat16 [768], P('shard'), may hold values from -2 to 2
- w_qkv: bfloat16 [768, 2304], P('shard'), may hold values from -0.3125 to 0.3125
- b_qkv: bfloat16 [2304], P('shard'), may hold values from -2 to 2
- w_attn: bfloat16 [768, 768], P('shard'), may hold values from -0.625 to 0.625
- b_attn: bfloat16 [768], P('shard'), may hold values from -2 to 2
- ln2_gain: bfloat16 [768], P('shard'), may hold values from 0.5 to 1.5
- ln2_bias: bfloat16 [768], P('shard'), may hold values from -2 to 2
- w_up: bfloat16 [768, 3072], P('shard'), may hold values from -0.21875 to 0.21875
- b_up: bfloat16 [3072], P('shard'), may hold values from -2 to 2
- w_down: bfloat16 [3072, 768], P('shard'), may hold values from -0.109375 to 0.109375
- b_down: bfloat16 [768], P('shard'), may hold values from -2 to 2
Outputs:
- mixed: float32 [32, 1024, 768], P(('replica', 'shard'))
- tokens_grad: float32 [32, 1024, 768], P(('replica', 'shard'))
- grad_ln1_gain: float32 [768], P('shard')
- grad_ln1_bias: float32 [768], P('shard')
- grad_w_qkv: float32 [768, 2304], P('shard')
- grad_b_qkv: float32 [2304], P('shard')
- grad_w_attn: float32 [768, 768], P('shard')
- grad_b_attn: float32 [768], P('shard')
- grad_ln2_gain: float32 [768], P('shard')
- grad_ln2_bias: float32 [768], P('shard')
- grad_w_up: float32 [768, 3072], P('shard')
- grad_b_up: float32 [3072], P('shard')
- grad_w_down: float32 [3072, 768], P('shard')
- grad_b_down: float32 [768], P('shard')
Inputs may be any that keep to these rules, and one draw needn't show every extreme that they name: `segments`: within each sequence the numbers never fall; each document spans 1 to 512 tokens, one of them exactly 512.
All inputs are finite; a program needn't handle non-finite values.
Results may differ from a plain program's by a relative error of at most 0.012.
The roundings to bfloat16 on the way count: a program that leaves them out, or rounds other values in their place, can miss the bound.
Values may be sent and summed in bfloat16 or wider, within the bound.
A program may use at most 320 MiB of HBM per device.

v0:
```python
import math

import jax
import jax.numpy as jnp
from jax import lax
from jax.sharding import PartitionSpec as P

HEADS = 12
HEAD = 64
ROT = 16


EPS = 1e-05
MASKED = -1e30
ROTARY_BASE = 10000.0


def layer_norm(inputs, gain, bias):
    average = jnp.mean(inputs, -1, keepdims=True)
    centered = inputs - average
    variance = jnp.mean(centered * centered, -1, keepdims=True)
    inv_scale = lax.rsqrt(variance + EPS)
    normal = centered * inv_scale
    return (normal * gain + bias, normal, inv_scale)


def norm_back(cotangent, normal, inv_scale, gain):
    scaled = cotangent * gain
    first_term = jnp.mean(scaled, -1, keepdims=True)
    second_term = jnp.mean(scaled * normal, -1, keepdims=True)
    return inv_scale * (scaled - first_term - normal * second_term)


def positions(segments):
    position_index = lax.broadcasted_iota(jnp.int32, segments.shape, segments.ndim - 1)
    first_flag = jnp.ones(segments.shape[:-1] + (1,), jnp.bool_)
    change = jnp.concatenate([first_flag, segments[..., 1:] != segments[..., :-1]], -1)
    doc_start = lax.cummax(jnp.where(change, position_index, 0), axis=segments.ndim - 1)
    return position_index - doc_start


def rotary_tables(places):
    half_width = ROT // 2
    frequency = ROTARY_BASE ** (-(jnp.arange(half_width, dtype=jnp.float32) * 2.0 / ROT))
    angles = places.astype(jnp.float32)[..., None] * frequency
    cosine = jnp.cos(angles)
    sine_table = jnp.sin(angles)
    return (jnp.concatenate([cosine, cosine], -1), jnp.concatenate([sine_table, sine_table], -1))


def rotate(field, cosine, sine_table):
    rotary_width = cosine.shape[-1]
    half_width = rotary_width // 2
    rotated_part = field[..., :rotary_width]
    turned = jnp.concatenate([-rotated_part[..., half_width:], rotated_part[..., :half_width]], -1)
    return jnp.concatenate(
        [rotated_part * cosine + turned * sine_table, field[..., rotary_width:]], -1
    )


def unrotate(cotangent, cosine, sine_table):
    rotary_width = cosine.shape[-1]
    half_width = rotary_width // 2
    rotated_part = cotangent[..., :rotary_width]
    moved_sin = rotated_part * sine_table
    back_turn = jnp.concatenate([moved_sin[..., half_width:], -moved_sin[..., :half_width]], -1)
    return jnp.concatenate([rotated_part * cosine + back_turn, cotangent[..., rotary_width:]], -1)


def gelu_slope(hidden):
    normal_cdf = 0.5 * (1.0 + lax.erf(hidden * (1.0 / math.sqrt(2.0))))
    density = jnp.exp(-0.5 * hidden * hidden) * (1.0 / math.sqrt(2.0 * math.pi))
    return normal_cdf + hidden * density


def block_scores(query_block, key_seq, seg_seq, offset):
    block_len = query_block.shape[0]
    key_len = key_seq.shape[0]
    scores = jnp.einsum(
        "qhd,khd->hqk", query_block, key_seq, preferred_element_type=jnp.float32
    ) * query_block.shape[-1] ** (-0.5)
    query_index = offset + lax.broadcasted_iota(jnp.int32, (block_len, key_len), 0)
    key_index = lax.broadcasted_iota(jnp.int32, (block_len, key_len), 1)
    seg_query = seg_seq[offset : offset + block_len]
    allowed = (seg_query[:, None] == seg_seq[None, :]) & (query_index >= key_index)
    return jnp.where(allowed[None], scores, MASKED)


def per_device(
    tokens,
    segments,
    out_grad,
    ln1_gain,
    ln1_bias,
    w_qkv,
    b_qkv,
    w_attn,
    b_attn,
    ln2_gain,
    ln2_bias,
    w_up,
    b_up,
    w_down,
    b_down,
):
    seq_count, length, width = tokens.shape
    total_rows = seq_count * length
    block_rows = min(512, length)
    head_scale = HEAD ** (-0.5)
    gathered = (
        lax.all_gather(ln1_gain, "shard", axis=0, tiled=True),
        lax.all_gather(ln1_bias, "shard", axis=0, tiled=True),
        lax.all_gather(w_qkv, "shard", axis=0, tiled=True),
        lax.all_gather(b_qkv, "shard", axis=0, tiled=True),
        lax.all_gather(w_attn, "shard", axis=0, tiled=True),
        lax.all_gather(b_attn, "shard", axis=0, tiled=True),
        lax.all_gather(ln2_gain, "shard", axis=0, tiled=True),
        lax.all_gather(ln2_bias, "shard", axis=0, tiled=True),
        lax.all_gather(w_up, "shard", axis=0, tiled=True),
        lax.all_gather(b_up, "shard", axis=0, tiled=True),
        lax.all_gather(w_down, "shard", axis=0, tiled=True),
        lax.all_gather(b_down, "shard", axis=0, tiled=True),
    )
    (
        gain_one,
        bias_one,
        full_qkv,
        bias_qkv,
        full_attn,
        bias_attn,
        gain_two,
        bias_two,
        full_up,
        bias_up,
        full_down,
        bias_down,
    ) = gathered
    inputs = tokens.reshape(total_rows, width).astype(jnp.float32)
    normed_one, normal_one, inv_one = layer_norm(
        inputs, gain_one.astype(jnp.float32), bias_one.astype(jnp.float32)
    )
    normed_one = normed_one.astype(jnp.bfloat16)
    normed_two, normal_two, inv_two = layer_norm(
        inputs, gain_two.astype(jnp.float32), bias_two.astype(jnp.float32)
    )
    normed_two = normed_two.astype(jnp.bfloat16)
    mixed_qkv = jnp.dot(normed_one, full_qkv, preferred_element_type=jnp.float32) + bias_qkv.astype(
        jnp.float32
    )
    qkv_parts = mixed_qkv.reshape(seq_count, length, 3, HEADS, HEAD)
    cosine, sine_table = rotary_tables(positions(segments))
    cosine = cosine[:, :, None, :]
    sine_table = sine_table[:, :, None, :]
    queries = rotate(qkv_parts[:, :, 0], cosine, sine_table).astype(jnp.bfloat16)
    key_rows = rotate(qkv_parts[:, :, 1], cosine, sine_table).astype(jnp.bfloat16)
    value_rows = qkv_parts[:, :, 2].astype(jnp.bfloat16)

    def attend_sequence(seq_items):
        query_seq, key_seq, value_seq, seg_seq = seq_items
        outputs = []
        log_parts = []
        for offset in range(0, length, block_rows):
            scores = block_scores(query_seq[offset : offset + block_rows], key_seq, seg_seq, offset)
            row_top = jnp.max(scores, -1, keepdims=True)
            exponent = jnp.exp(scores - row_top)
            row_total = jnp.sum(exponent, -1, keepdims=True)
            probabilities = (exponent / row_total).astype(jnp.bfloat16)
            outputs.append(
                jnp.einsum(
                    "hqk,khd->qhd", probabilities, value_seq, preferred_element_type=jnp.float32
                )
            )
            log_parts.append(row_top + jnp.log(row_total))
        return (jnp.concatenate(outputs, 0), jnp.concatenate(log_parts, 1))

    attended, log_totals = lax.map(attend_sequence, (queries, key_rows, value_rows, segments))
    context = attended.reshape(total_rows, width).astype(jnp.bfloat16)
    attn_out = jnp.dot(context, full_attn, preferred_element_type=jnp.float32) + bias_attn.astype(
        jnp.float32
    )
    hidden = jnp.dot(normed_two, full_up, preferred_element_type=jnp.float32) + bias_up.astype(
        jnp.float32
    )
    activated = jax.nn.gelu(hidden, approximate=False).astype(jnp.bfloat16)
    mlp_out = jnp.dot(activated, full_down, preferred_element_type=jnp.float32) + bias_down.astype(
        jnp.float32
    )
    mixed = inputs + attn_out + mlp_out
    back_qkv, back_attn, back_up, back_down, back_gain_one, back_gain_two = (
        lax.all_gather(w_qkv, "shard", axis=0, tiled=True),
        lax.all_gather(w_attn, "shard", axis=0, tiled=True),
        lax.all_gather(w_up, "shard", axis=0, tiled=True),
        lax.all_gather(w_down, "shard", axis=0, tiled=True),
        lax.all_gather(ln1_gain, "shard", axis=0, tiled=True),
        lax.all_gather(ln2_gain, "shard", axis=0, tiled=True),
    )
    grad_rows = out_grad.reshape(total_rows, width)
    grad_float = grad_rows.astype(jnp.float32)
    grad_b_attn = jnp.sum(grad_float, 0)
    grad_w_attn = jnp.einsum("rd,re->de", context, grad_rows, preferred_element_type=jnp.float32)
    grad_w_down = jnp.einsum("rf,re->fe", activated, grad_rows, preferred_element_type=jnp.float32)
    grad_context = jnp.einsum(
        "re,de->rd", grad_rows, back_attn, preferred_element_type=jnp.float32
    ).astype(jnp.bfloat16)
    grad_act = jnp.einsum("re,fe->rf", grad_rows, back_down, preferred_element_type=jnp.float32)
    grad_hidden = (grad_act * gelu_slope(hidden)).astype(jnp.bfloat16)
    grad_b_up = jnp.sum(grad_hidden.astype(jnp.float32), 0)
    grad_w_up = jnp.einsum("rd,rf->df", normed_two, grad_hidden, preferred_element_type=jnp.float32)
    grad_normed_two = jnp.einsum(
        "rf,df->rd", grad_hidden, back_up, preferred_element_type=jnp.float32
    )
    grad_context_seq = grad_context.reshape(seq_count, length, HEADS, HEAD)

    def attend_back(seq_items):
        query_seq, key_seq, value_seq, seg_seq, log_seq, grad_seq = seq_items
        query_grads = []
        key_grads = jnp.zeros(key_seq.shape, jnp.float32)
        value_grads = jnp.zeros(value_seq.shape, jnp.float32)
        for offset in range(0, length, block_rows):
            query_block = query_seq[offset : offset + block_rows]
            grad_block = grad_seq[offset : offset + block_rows]
            scores = block_scores(query_block, key_seq, seg_seq, offset)
            probabilities = jnp.exp(scores - log_seq[:, offset : offset + block_rows])
            grad_probs = jnp.einsum(
                "qhd,khd->hqk", grad_block, value_seq, preferred_element_type=jnp.float32
            )
            inner_sum = jnp.sum(probabilities * grad_probs, -1, keepdims=True)
            grad_scores = (probabilities * (grad_probs - inner_sum)).astype(jnp.bfloat16)
            value_grads = value_grads + jnp.einsum(
                "hqk,qhd->khd",
                probabilities.astype(jnp.bfloat16),
                grad_block,
                preferred_element_type=jnp.float32,
            )
            query_grads.append(
                jnp.einsum("hqk,khd->qhd", grad_scores, key_seq, preferred_element_type=jnp.float32)
                * head_scale
            )
            key_grads = (
                key_grads
                + jnp.einsum(
                    "hqk,qhd->khd", grad_scores, query_block, preferred_element_type=jnp.float32
                )
                * head_scale
            )
        return (jnp.concatenate(query_grads, 0), key_grads, value_grads)

    grad_queries, grad_keys, grad_values = lax.map(
        attend_back, (queries, key_rows, value_rows, segments, log_totals, grad_context_seq)
    )
    grad_queries = unrotate(grad_queries, cosine, sine_table)
    grad_keys = unrotate(grad_keys, cosine, sine_table)
    grad_mixed_qkv = (
        jnp.stack([grad_queries, grad_keys, grad_values], 2)
        .reshape(total_rows, 3 * width)
        .astype(jnp.bfloat16)
    )
    grad_b_qkv = jnp.sum(grad_mixed_qkv.astype(jnp.float32), 0)
    grad_w_qkv = jnp.einsum(
        "rd,rc->dc", normed_one, grad_mixed_qkv, preferred_element_type=jnp.float32
    )
    grad_normed_one = jnp.einsum(
        "rc,dc->rd", grad_mixed_qkv, back_qkv, preferred_element_type=jnp.float32
    )
    grad_ln1_gain = jnp.sum(grad_normed_one * normal_one, 0)
    grad_ln1_bias = jnp.sum(grad_normed_one, 0)
    grad_ln2_gain = jnp.sum(grad_normed_two * normal_two, 0)
    grad_ln2_bias = jnp.sum(grad_normed_two, 0)
    tokens_grad = (
        grad_float
        + norm_back(grad_normed_one, normal_one, inv_one, back_gain_one.astype(jnp.float32))
        + norm_back(grad_normed_two, normal_two, inv_two, back_gain_two.astype(jnp.float32))
    )
    gradients = (
        grad_ln1_gain,
        grad_ln1_bias,
        grad_w_qkv,
        grad_b_qkv,
        grad_w_attn,
        grad_b_attn,
        grad_ln2_gain,
        grad_ln2_bias,
        grad_w_up,
        grad_b_up,
        grad_w_down,
        grad_b_attn,
    )
    owned = (
        lax.psum_scatter(
            gradients[0].astype(jnp.bfloat16), "shard", scatter_dimension=0, tiled=True
        ).astype(jnp.float32),
        lax.psum_scatter(
            gradients[1].astype(jnp.bfloat16), "shard", scatter_dimension=0, tiled=True
        ).astype(jnp.float32),
        lax.psum_scatter(
            gradients[2].astype(jnp.bfloat16), "shard", scatter_dimension=0, tiled=True
        ).astype(jnp.float32),
        lax.psum_scatter(
            gradients[3].astype(jnp.bfloat16), "shard", scatter_dimension=0, tiled=True
        ).astype(jnp.float32),
        lax.psum_scatter(
            gradients[4].astype(jnp.bfloat16), "shard", scatter_dimension=0, tiled=True
        ).astype(jnp.float32),
        lax.psum_scatter(
            gradients[5].astype(jnp.bfloat16), "shard", scatter_dimension=0, tiled=True
        ).astype(jnp.float32),
        lax.psum_scatter(
            gradients[6].astype(jnp.bfloat16), "shard", scatter_dimension=0, tiled=True
        ).astype(jnp.float32),
        lax.psum_scatter(
            gradients[7].astype(jnp.bfloat16), "shard", scatter_dimension=0, tiled=True
        ).astype(jnp.float32),
        lax.psum_scatter(
            gradients[8].astype(jnp.bfloat16), "shard", scatter_dimension=0, tiled=True
        ).astype(jnp.float32),
        lax.psum_scatter(
            gradients[9].astype(jnp.bfloat16), "shard", scatter_dimension=0, tiled=True
        ).astype(jnp.float32),
        lax.psum_scatter(
            gradients[10].astype(jnp.bfloat16), "shard", scatter_dimension=0, tiled=True
        ).astype(jnp.float32),
        lax.psum_scatter(
            gradients[11].astype(jnp.bfloat16), "shard", scatter_dimension=0, tiled=True
        ).astype(jnp.float32),
    )
    reduced = lax.psum(
        (
            owned[0],
            owned[1],
            owned[2],
            owned[3],
            owned[4],
            owned[5],
            owned[6],
            owned[7],
            owned[8],
            owned[9],
            owned[10],
            owned[11],
        ),
        "replica",
    )
    return (
        mixed.reshape(seq_count, length, width),
        tokens_grad.reshape(seq_count, length, width),
        reduced[0],
        reduced[1],
        reduced[2],
        reduced[3],
        reduced[4],
        reduced[5],
        reduced[6],
        reduced[7],
        reduced[8],
        reduced[9],
        reduced[10],
        reduced[11],
    )


def solution(mesh):
    in_specs = (
        P(("replica", "shard"), None, None),
        P(("replica", "shard"), None),
        P(("replica", "shard"), None, None),
        P("shard"),
        P("shard"),
        P("shard", None),
        P("shard"),
        P("shard", None),
        P("shard"),
        P("shard"),
        P("shard"),
        P("shard", None),
        P("shard"),
        P("shard", None),
        P("shard"),
    )
    out_specs = (
        P(("replica", "shard"), None, None),
        P(("replica", "shard"), None, None),
        P("shard"),
        P("shard"),
        P("shard", None),
        P("shard"),
        P("shard", None),
        P("shard"),
        P("shard"),
        P("shard"),
        P("shard", None),
        P("shard"),
        P("shard", None),
        P("shard"),
    )
    return jax.shard_map(
        per_device, mesh=mesh, in_specs=in_specs, out_specs=out_specs, check_vma=False
    )
```

profile of v0, /device:TPU:0, one launch (start us, length us, event | category | flops | bytes accessed | tf_op | source)
XLA Modules:
  0.0 760.1 jit_solution(8639375350140645876)
XLA Ops:
  7.3 0.7 all-gather.8.cloned.1.call-update
  8.1 0.7 all-gather.6.cloned.1.call-update
  8.8 0.7 all-gather.10.cloned.1.call-update
  9.5 0.5 all-gather.12.cloned.1.call-update
  10.3 0.6 fusion.132
  13.4 13.1 %all-reduce.16 = (bf16[768]{0:T(1024)(128)(2,1)S(1)}, bf16[768]{0:T(1024)(128)(2,1)S(1)}, bf16[2304]{0:T(1024)(128)(2,1)S(1)}, bf16[768]{0:T(1024)(128)(2,1)S(1)}, bf16[768]{0:T(1024)(128)(2,1)S(1)}) all-reduce(bf16[768]{0:T(1024)(128)(2,1)S(1)} %dynamic-update-slice.5, ...), channel_id=1, replica_groups=mesh['replica'=8,'shard'=4] {'shard'}, use_global_device_ids=true, to_apply=%add.5 | all-reduce | flops 5376 | bytes 21504
  26.9 0.6 fusion.57
  27.6 0.3 reduce-window.6
  28.6 0.6 convert_element_type.211
  29.2 0.6 convert_element_type.212
  29.8 5.5 all-gather
  35.3 0.6 convert_element_type.247
  35.9 1.7 fusion.64
  37.6 3.4 convolution_convert_fusion.3
  41.1 1.2 fusion.128
  42.3 20.1 %all-gather.6.cloned.1.call-done = bf16[768,2304]{1,0:T(8,128)(2,1)} async-done(((bf16[192,2304]{1,0:T(8,128)(2,1)}), bf16[768,2304]{1,0:T(8,128)(2,1)}) %all-gather.6.cloned.1.call-update) | async-done | bytes 3538960 | tf_op jit(solution)/shard_map/all_gather | solution.py:113
  62.4 8.7 %convolution_add_fusion = f32[1024,2304]{1,0:T(8,128)} fusion(bf16[768,2304]{1,0:T(8,128)(2,1)} %all-gather.6.cloned.1.call-done, f32[2304]{0:T(1024)S(1)} %convert_element_type.204, bf16[1,1024,768]{2,1,0:T(8,128)(2,1)S(1)} %copy-done, f32[768]{0:T(1024)S(1)} %convert_element_type.202, f32[768]{0:T(1024)S(1)} %convert_element_type.201, ...), kind=kOutput, calls=%fused_computation.51 | convolution fusion | flops 3630956544 | bytes 14572544 | tf_op jit(solution)/shard_map/dot_general | solution.py:147
  71.0 9.8 %copy.33 = f32[1024,2304]{0,1:T(8,128)} copy(f32[1024,2304]{1,0:T(8,128)} %convolution_add_fusion) | data formatting | bytes 18874368 | tf_op jit(solution)/shard_map/add | solution.py:147
  80.8 3.5 slice_bitcast_fusion
  84.9 0.4 fusion.103
  85.3 0.5 copy-done.2
  85.7 10.7 %fusion.28 = (f32[12,512]{1,0:T(8,128)S(1)}, f32[12,512,1024]{2,1,0:T(8,128)}) fusion(pred[512,1024]{1,0:T(8,128)(4,1)S(1)} %copy-done.2, bf16[1024,12,48]{0,2,1:T(8,128)(2,1)S(1)} %fusion.95, bf16[1024,12,16]{0,2,1:T(8,128)(2,1)S(1)} %get-tuple-element.116, bf16[1,1024,12,16]{1,3,2,0:T(8,128)(2,1)S(1)} %get-tuple-element.117, ...), kind=kOutput, calls=%fused_computation.49 | convolution fusion | flops 828893184 | bytes 28860416 | tf_op jit(solution)/shard_map/while/body/eval_jaxpr/qhd,khd->hqk/dot_general | solution.py:79
  96.4 11.8 %fusion = f32[12,512]{1,0:T(8,128)S(1)} fusion(f32[12,512]{1,0:T(8,128)S(1)} %get-tuple-element.134, f32[12,512,1024]{2,1,0:T(8,128)} %get-tuple-element.135, pred[512,1024]{1,0:T(8,128)(4,1)S(1)} %copy-done.2), kind=kLoop, calls=%fused_computation.12 | loop fusion | flops 25159680 | bytes 25739264 | tf_op jit(solution)/shard_map/while/body/eval_jaxpr/reduce_sum | solution.py:166
  108.3 11.2 %fusion.29 = (f32[12,512]{1,0:T(8,128)S(1)}, f32[12,512,1024]{2,1,0:T(8,128)}) fusion(pred[512,1024]{1,0:T(8,128)(4,1)S(1)} %get-tuple-element.125, bf16[1024,12,48]{0,2,1:T(8,128)(2,1)S(1)} %fusion.95, bf16[1024,12,16]{0,2,1:T(8,128)(2,1)S(1)} %get-tuple-element.116, bf16[1,1024,12,48]{1,3,2,0:T(8,128)(2,1)S(1)} %slice.227, ...), kind=kOutput, calls=%fused_computation.50 | convolution fusion | flops 828893184 | bytes 28860416 | tf_op jit(solution)/shard_map/while/body/eval_jaxpr/qhd,khd->hqk/dot_general | solution.py:79
  119.5 12.4 %fusion.1 = f32[12,512]{1,0:T(8,128)S(1)} fusion(f32[12,512]{1,0:T(8,128)S(1)} %get-tuple-element.132, f32[12,512,1024]{2,1,0:T(8,128)} %get-tuple-element.133, pred[512,1024]{1,0:T(8,128)(4,1)S(1)} %get-tuple-element.125), kind=kLoop, calls=%fused_computation.13 | loop fusion | flops 25159680 | bytes 25739264 | tf_op jit(solution)/shard_map/while/body/eval_jaxpr/reduce_sum | solution.py:166
  131.9 0.6 copy-done.27
  132.5 18.7 %multiply_reduce_fusion.1 = (f32[12,512]{1,0:T(8,128)S(1)}, f32[12,512,1024]{2,1,0:T(8,128)}) fusion(f32[12,512]{1,0:T(8,128)S(1)} %log_add_fusion.1, f32[12,512,1024]{2,1,0:T(8,128)} %get-tuple-element.135, pred[512,1024]{1,0:T(8,128)(4,1)} %get-tuple-element.124, bf16[512,12,64]{0,2,1:T(8,128)(2,1)} %bitcast.202, f32[1,1024,3,12,64]{1,4,3,2,0:T(8,128)} %bitcast.194), kind=kOutput, calls=%fused_computation.4 | convolution fusion | flops 836757504 | bytes 53264384 | tf_op jit(solution)/shard_map/while/body/eval_jaxpr/qhd,khd->hqk/dot_general | solution.py:224
  151.2 18.5 %multiply_reduce_fusion = (f32[12,512]{1,0:T(8,128)S(1)}, f32[12,512,1024]{2,1,0:T(8,128)}) fusion(f32[12,512]{1,0:T(8,128)S(1)} %log_add_fusion, f32[12,512,1024]{2,1,0:T(8,128)} %get-tuple-element.133, pred[512,1024]{1,0:T(8,128)(4,1)S(1)} %get-tuple-element.125, bf16[512,12,64]{0,2,1:T(8,128)(2,1)} %bitcast.204, f32[1,1024,3,12,64]{1,4,3,2,0:T(8,128)} %bitcast.195), kind=kOutput, calls=%fused_computation.1 | convolution fusion | flops 836757504 | bytes 53264384 | tf_op jit(solution)/shard_map/while/body/eval_jaxpr/qhd,khd->hqk/dot_general | solution.py:224
  169.8 42.1 %multiply_convert_fusion = (bf16[12,512,1024]{2,1,0:T(8,128)(2,1)}, bf16[12,512,1024]{2,1,0:T(8,128)(2,1)}) fusion(f32[12,512,1024]{2,1,0:T(8,128)} %get-tuple-element.139, f32[12,512]{1,0:T(8,128)S(1)} %get-tuple-element.138, f32[12,512]{1,0:T(8,128)S(1)} %log_add_fusion, f32[12,512,1024]{2,1,0:T(8,128)} %get-tuple-element.133, ...), kind=kLoop, calls=%fused_computation | loop fusion | flops 75497472 | bytes 126976000 | tf_op jit(solution)/shard_map/while/body/eval_jaxpr/convert_element_type | solution.py:228
  211.9 9.8 %multiply_bitcast_fusion.2 = f32[512,12,64]{0,2,1:T(8,128)} fusion(bf16[12,512,1024]{2,1,0:T(8,128)(2,1)} %get-tuple-element.144, bf16[1024,12,48]{0,2,1:T(8,128)(2,1)S(1)} %fusion.95, bf16[1024,12,16]{0,2,1:T(8,128)(2,1)S(1)} %get-tuple-element.116), kind=kOutput, calls=%fused_computation.128 | convolution fusion | flops 808845312 | bytes 15728640 | tf_op jit(solution)/shard_map/while/body/eval_jaxpr/hqk,khd->qhd/dot_general | solution.py:236
  221.7 7.1 fusion.121
  228.9 12.9 %fusion.94 = bf16[12,64,512]{2,1,0:T(8,128)(2,1)} fusion(f32[12,512]{1,0:T(8,128)S(1)} %fusion, f32[12,512]{1,0:T(8,128)S(1)} %get-tuple-element.134, f32[12,512,1024]{2,1,0:T(8,128)} %get-tuple-element.135, pred[512,1024]{1,0:T(8,128)(4,1)S(1)} %copy-done.3, f32[1,1024,3,12,64]{1,4,3,2,0:T(8,128)S(1)} %bitcast.199), kind=kOutput, calls=%fused_computation.135 | convolution fusion | flops 837156864 | bytes 28114944 | tf_op jit(solution)/shard_map/while/body/eval_jaxpr/hqk,khd->qhd/dot_general | solution.py:169
  241.8 8.7 %multiply_bitcast_fusion.1 = f32[512,12,64]{0,2,1:T(8,128)S(1)} fusion(bf16[12,512,1024]{2,1,0:T(8,128)(2,1)} %get-tuple-element.143, bf16[1024,12,48]{0,2,1:T(8,128)(2,1)S(1)} %fusion.95, bf16[1024,12,16]{0,2,1:T(8,128)(2,1)} %copy-done.7), kind=kOutput, calls=%fused_computation.127 | convolution fusion | flops 808845312 | bytes 15728640 | tf_op jit(solution)/shard_map/while/body/eval_jaxpr/hqk,khd->qhd/dot_general | solution.py:236
  250.6 7.2 multiply_bitcast_fusion
  257.8 0.3 maximum_bitcast_fusion
  258.1 1.4 copy-done.22
  260.1 0.5 copy-done.20
  260.6 0.4 maximum_add_fusion
  261.0 1.3 maximum_bitcast_fusion.1
  262.2 1.3 maximum_bitcast_fusion.2
  263.8 9.5 %fusion.93 = bf16[12,64,512]{2,1,0:T(8,128)(2,1)} fusion(f32[12,512]{1,0:T(8,128)S(1)} %copy-done.28, f32[12,512]{1,0:T(8,128)S(1)} %copy-done.26, f32[12,512,1024]{2,1,0:T(8,128)S(1)} %bitcast.192, pred[512,1024]{1,0:T(8,128)(4,1)S(1)} %get-tuple-element.125, f32[1,1024,3,12,64]{1,4,3,2,0:T(8,128)} %bitcast.196), kind=kOutput, calls=%fused_computation.134 | convolution fusion | flops 837156864 | bytes 28098560 | tf_op jit(solution)/shard_map/while/body/eval_jaxpr/hqk,khd->qhd/dot_general | solution.py:169
  273.3 4.4 fusion.88
  277.6 13.5 %fusion.13 = f32[12,64,1024]{2,1,0:T(8,128)} fusion(bf16[512,12,64]{0,2,1:T(8,128)(2,1)S(1)} %bitcast.205, f32[12,512]{1,0:T(8,128)S(1)} %log_add_fusion, f32[12,512,1024]{2,1,0:T(8,128)} %get-tuple-element.133, pred[512,1024]{1,0:T(8,128)(4,1)S(1)} %get-tuple-element.125), kind=kOutput, calls=%fused_computation.27 | convolution fusion | flops 830472192 | bytes 29646848 | tf_op jit(solution)/shard_map/while/body/eval_jaxpr/hqk,qhd->khd/dot_general | solution.py:229
  291.3 13.4 %add_bitcast_fusion = bf16[1,1024,1,12,64]{1,4,3,2,0:T(8,128)(2,1)S(1)} fusion(f32[12,64,1024]{2,1,0:T(8,128)} %fusion.13, bf16[512,12,64]{0,2,1:T(8,128)(2,1)S(1)} %bitcast.203, f32[12,512]{1,0:T(8,128)S(1)} %copy-done.24, f32[12,512,1024]{2,1,0:T(8,128)} %get-tuple-element.135, pred[512,1024]{1,0:T(8,128)(4,1)S(1)} %copy-done.4), kind=kOutput, calls=%fused_computation.98 | convolution fusion | flops 832045056 | bytes 31219712 | tf_op jit(solution)/shard_map/while/body/eval_jaxpr/hqk,qhd->khd/dot_general | solution.py:229
  304.7 0.8 fusion.127
  305.6 2.2 copy-done.12
  307.8 6.0 convolution_convert_fusion.2
  313.9 0.6 copy-done.36
  314.5 37.4 %fusion.6 = (bf16[1024,3072]{1,0:T(8,128)(2,1)}, f32[1024,3072]{1,0:T(8,128)}) fusion(f32[3072]{0:T(1024)S(1)} %bitcast.213, bf16[768,3072]{1,0:T(8,128)(2,1)} %all-gather.10.cloned.1.call-done, bf16[1,1024,768]{2,1,0:T(8,128)(2,1)S(1)} %copy-done.1, f32[768]{0:T(1024)S(1)} %copy-done.40, f32[768]{0:T(1024)S(1)} %copy-done.36, f32[1024]{0:T(1024)S(1)} %copy-done.35, ...), kind=kOutput, calls=%fused_computation.20 | convolution fusion | flops 5044174848 | bytes 25192448 | tf_op jit(solution)/shard_map/dot_general | solution.py:181
  351.9 11.8 %fusion.133 = (bf16[3072]{0:T(1024)(128)(2,1)S(1)}, bf16[1024,3072]{1,0:T(8,128)(2,1)S(1)}) fusion(f32[1024,3072]{1,0:T(8,128)} %get-tuple-element.131, f32[3072]{0:T(1024)S(1)} %bitcast.214, bf16[3072,768]{1,0:T(8,128)(2,1)} %all-gather.12.cloned.1.call-done, bf16[1,1024,768]{2,1,0:T(8,128)(2,1)S(1)} %copy-done.8), kind=kOutput, calls=%fused_computation.208 | convolution fusion | flops 4869583872 | bytes 25184256 | tf_op jit(solution)/shard_map/re,fe->rf/dot_general | solution.py:205
  363.7 2.6 copy-done.53
  366.3 7.7 %convolution_convert_fusion.1 = bf16[768,3072]{1,0:T(8,128)(2,1)} fusion(bf16[1024,3072]{1,0:T(8,128)(2,1)S(1)} %get-tuple-element.142, bf16[1,1024,768]{2,1,0:T(8,128)(2,1)S(1)} %copy-done.1, f32[768]{0:T(1024)S(1)} %copy-done.40, f32[768]{0:T(1024)S(1)} %copy-done.36, f32[1024]{0:T(1024)S(1)} %copy-done.35, f32[1024]{0:T(1024)S(1)} %copy-done.31), kind=kOutput, calls=%fused_computation.53 | convolution fusion | flops 4838916096 | bytes 12597248 | tf_op jit(solution)/shard_map/rd,rf->df/dot_general | solution.py:208
  374.1 10.0 %convolution_convert_fusion = bf16[3072,768]{1,0:T(8,128)(2,1)} fusion(bf16[1024,3072]{1,0:T(8,128)(2,1)} %get-tuple-element.130, bf16[1,1024,768]{2,1,0:T(8,128)(2,1)S(1)} %copy-done.8), kind=kOutput, calls=%fused_computation.52 | convolution fusion | flops 4834197504 | bytes 12582912 | tf_op jit(solution)/shard_map/rf,re->fe/dot_general | solution.py:201
  384.1 0.3 reduce_sum.190
  386.9 2.7 pad_maximum_fusion.1
  389.6 8.7 %fusion.139 = f32[1024,768]{1,0:T(8,128)S(1)} fusion(bf16[1024,3072]{1,0:T(8,128)(2,1)} %copy-done.53, bf16[768,3072]{1,0:T(8,128)(2,1)} %all-gather.10.cloned.1.call-done), kind=kOutput, calls=%fused_computation.210 | convolution fusion | flops 4831838208 | bytes 14155776 | tf_op jit(solution)/shard_map/rf,df->rd/dot_general | solution.py:209
  398.3 10.7 %fusion.55 = (bf16[768]{0:T(1024)(128)(2,1)S(1)}, f32[1024]{0:T(1024)S(1)}, f32[1024]{0:T(1024)S(1)}, bf16[768]{0:T(1024)(128)(2,1)S(1)}, bf16[768]{0:T(1024)(12...) fusion(bf16[1,1024,768]{2,1,0:T(8,128)(2,1)S(1)} %copy-done.1, ...), kind=kOutput, calls=%fused_computation.83 | convolution fusion | flops 3637240832 | bytes 16158720 | tf_op jit(solution)/shard_map/rc,dc->rd/dot_general | solution.py:262
  409.1 12.3 %all-reduce.15 = (bf16[768]{0:T(1024)(128)(2,1)S(1)}, bf16[768]{0:T(1024)(128)(2,1)S(1)}, bf16[768]{0:T(1024)(128)(2,1)S(1)}, bf16[768]{0:T(1024)(128)(2,1)S(1)}...) all-reduce(bf16[768]{0:T(1024)(128)(2,1)S(1)} %dynamic-update-slice, ...), channel_id=1, replica_groups=mesh['replica'=8,'shard'=4] {'shard'}, use_global_device_ids=true, to_apply=%add.6 | all-reduce | flops 10752 | bytes 43008
  421.9 8.7 %fusion.138 = f32[1024,768]{1,0:T(8,128)S(1)} fusion(bf16[1024,3072]{1,0:T(8,128)(2,1)} %get-tuple-element.130, bf16[3072,768]{1,0:T(8,128)(2,1)} %all-gather.12.cloned.1.call-done), kind=kOutput, calls=%fused_computation.209 | convolution fusion | flops 4831838208 | bytes 14155776 | tf_op jit(solution)/shard_map/dot_general | solution.py:185
  430.7 3.7 fusion.59
  434.6 3.3 fusion.51
  437.8 35.6 %reduce-scatter.11.cloned.1.call-done = bf16[768,768]{1,0:T(8,128)(2,1)} async-done(((bf16[3072,768]{1,0:T(8,128)(2,1)}), bf16[768,768]{1,0:T(8,128)(2,1)}) %reduce-scatter.11.cloned.1.call-update) | async-done | bytes 1179664 | tf_op jit(solution)/shard_map/reduce_scatter | solution.py:319
  473.4 279.1 %all-reduce.18 = (f32[192]{0:T(256)}, f32[192]{0:T(256)}, f32[192,2304]{1,0:T(8,128)}, f32[576]{0:T(1024)}, f32[192,768]{1,0:T(8,128)}, /*index=5*/f32[192]{0:T(...) all-reduce(f32[192]{0:T(256)S(1)} %dynamic-slice_convert_fusion.6, ...), channel_id=1, replica_groups=mesh['replica'=8,'shard'=4] {'replica'}, use_global_device_ids=true, to_apply=%region_16.17 | all-reduce | flops 1771776 | bytes 10635264 | tf_op jit(solution)/shard_map/psum | solution.py:326
  752.4 0.6 copy.58
  (199 shorter events, 5.7 us)
Async XLA Ops:
  7.2 3.1 copy-start.41
  7.2 3.0 copy-start.29
  7.2 5.0 copy-start.47
  7.2 5.2 copy-start.48
  7.2 5.4 copy-start.49
  7.2 5.7 copy-start.50
  7.2 5.9 copy-start.42
  7.3 19.3 %copy-start = (bf16[1,1024,768]{2,1,0:T(8,128)(2,1)S(1)}, bf16[1,1024,768]{2,1,0:T(8,128)(2,1)}, u32[]{:S(2)}) copy-start(bf16[1,1024,768]{2,1,0:T(8,128)(2,1)} %param.15) | copy-start | bytes 4718596
  7.3 22.5 %copy-start.43 = (bf16[768]{0:T(1024)(128)(2,1)S(1)}, bf16[768]{0:T(1024)(128)(2,1)}, u32[]{:S(2)}) copy-start(bf16[768]{0:T(1024)(128)(2,1)} %param.27) | copy-start | bytes 4612
  7.3 30.3 %all-gather.8.cloned.1.call-start = ((), (), s32[]{:S(2)}) async-start(), calls=%async_computation.5 | async-start | bytes 1474560 | tf_op jit(solution)/shard_map/all_gather | solution.py:115
  8.0 54.4 %all-gather.6.cloned.1.call-start = ((), (), s32[]{:S(2)}) async-start(), calls=%async_computation.4 | async-start | bytes 4423680 | tf_op jit(solution)/shard_map/all_gather | solution.py:113
  8.8 305.1 %all-gather.10.cloned.1.call-start = ((), (), s32[]{:S(2)}) async-start(), calls=%async_computation.6 | async-start | bytes 5898240 | tf_op jit(solution)/shard_map/all_gather | solution.py:119
  9.5 342.4 %all-gather.12.cloned.1.call-start = ((), (), s32[]{:S(2)}) async-start(), calls=%async_computation.7 | async-start | bytes 5898240 | tf_op jit(solution)/shard_map/all_gather | solution.py:121
  10.1 427.7 %reduce-scatter.7.cloned.1.call-start = ((), (), s32[]{:S(2)}) async-start(), calls=%async_computation.9 | async-start | bytes 1474560 | tf_op jit(solution)/shard_map/reduce_scatter | solution.py:301
  26.5 35.8 %copy-start.32 = (f32[768]{0:T(1024)}, f32[768]{0:T(1024)S(1)}, u32[]{:S(2)}) copy-start(f32[768]{0:T(1024)S(1)} %convert_element_type.201) | copy-start | bytes 9220
  26.5 35.8 %copy-start.38 = (f32[768]{0:T(1024)}, f32[768]{0:T(1024)S(1)}, u32[]{:S(2)}) copy-start(f32[768]{0:T(1024)S(1)} %convert_element_type.202) | copy-start | bytes 9220
  26.9 35.5 %copy-start.30 = (f32[1024]{0:T(1024)}, f32[1024]{0:T(1024)S(1)}, u32[]{:S(2)}) copy-start(f32[1024]{0:T(1024)S(1)} %broadcast_multiply_fusion.4) | copy-start | bytes 12292
  27.5 34.9 %copy-start.34 = (f32[1024]{0:T(1024)}, f32[1024]{0:T(1024)S(1)}, u32[]{:S(2)}) copy-start(f32[1024]{0:T(1024)S(1)} %add_rsqrt_fusion) | copy-start | bytes 12292
  28.6 56.3 %copy-start.19 = (f32[1024,16]{0,1:T(8,128)}, f32[1024,16]{0,1:T(8,128)S(1)}, u32[]{:S(2)}) copy-start(f32[1024,16]{0,1:T(8,128)S(1)} %maximum_bitcast_fusion.3) | copy-start | bytes 196612
  28.6 56.3 %copy-start.21 = (f32[1024,16]{0,1:T(8,128)}, f32[1024,16]{0,1:T(8,128)S(1)}, u32[]{:S(2)}) copy-start(f32[1024,16]{0,1:T(8,128)S(1)} %maximum_bitcast_fusion.4) | copy-start | bytes 196612
  85.2 23.1 %copy-start.5 = (bf16[1,1024,12,16]{1,3,2,0:T(8,128)(2,1)}, bf16[1,1024,12,16]{1,3,2,0:T(8,128)(2,1)S(1)}, u32[]{:S(2)}) copy-start(bf16[1,1024,12,16]{1,3,2,0:T(8,128)(2,1)S(1)} %get-tuple-element.117) | copy-start | bytes 1179652
  85.2 126.6 %copy-start.7 = (bf16[1024,12,16]{0,2,1:T(8,128)(2,1)}, bf16[1024,12,16]{0,2,1:T(8,128)(2,1)S(1)}, u32[]{:S(2)}) copy-start(bf16[1024,12,16]{0,2,1:T(8,128)(2,1)S(1)} %get-tuple-element.116) | copy-start | bytes 1179652
  108.3 61.5 %copy-start.23 = (f32[12,512]{1,0:T(8,128)}, f32[12,512]{1,0:T(8,128)S(1)}, u32[]{:S(2)}) copy-start(f32[12,512]{1,0:T(8,128)S(1)} %log_add_fusion.1) | copy-start | bytes 73732
  119.5 12.4 %copy-start.25 = (f32[12,512]{1,0:T(8,128)}, f32[12,512]{1,0:T(8,128)S(1)}, u32[]{:S(2)}) copy-start(f32[12,512]{1,0:T(8,128)S(1)} %get-tuple-element.132) | copy-start | bytes 73732
  211.9 16.9 %slice-start.6 = ((s8[9437184]{0:T(1024)(128)(4,1)}), s8[1048576]{0:T(1024)(128)(4,1)S(1)}, s32[]{:S(2)}) async-start(s8[9437184]{0:T(1024)(128)(4,1)} %bitcast.197), calls=%async_computation.18 | async-start | bytes 2097152
  211.9 16.9 %slice-start.7 = ((s8[9437184]{0:T(1024)(128)(4,1)}), s8[4194304]{0:T(1024)(128)(4,1)S(1)}, s32[]{:S(2)}) async-start(s8[9437184]{0:T(1024)(128)(4,1)} %bitcast.197), calls=%async_computation.19 | async-start | bytes 8388608
  221.7 7.1 slice-start.8
  221.7 7.2 copy-start.3
  241.8 8.7 %copy-start.6 = (bf16[1,1024,12,16]{1,3,2,0:T(8,128)(2,1)S(1)}, bf16[1,1024,12,16]{1,3,2,0:T(8,128)(2,1)}, u32[]{:S(2)}) copy-start(bf16[1,1024,12,16]{1,3,2,0:T(8,128)(2,1)} %copy-done.5) | copy-start | bytes 1179652
  250.5 7.3 copy-start.11
  250.5 13.0 %slice-start = ((s8[25165824]{0:T(1024)(128)(4,1)}), s8[4194304]{0:T(1024)(128)(4,1)S(1)}, s32[]{:S(2)}) async-start(s8[25165824]{0:T(1024)(128)(4,1)} %bitcast.191), calls=%async_computation.12 | async-start | bytes 8388608
  250.5 13.0 %slice-start.1 = ((s8[25165824]{0:T(1024)(128)(4,1)}), s8[4194304]{0:T(1024)(128)(4,1)S(1)}, s32[]{:S(2)}) async-start(s8[25165824]{0:T(1024)(128)(4,1)} %bitcast.191), calls=%async_computation.13 | async-start | bytes 8388608
  250.5 13.0 %slice-start.2 = ((s8[25165824]{0:T(1024)(128)(4,1)}), s8[4194304]{0:T(1024)(128)(4,1)S(1)}, s32[]{:S(2)}) async-start(s8[25165824]{0:T(1024)(128)(4,1)} %bitcast.191), calls=%async_computation.14 | async-start | bytes 8388608
  250.5 13.0 %slice-start.3 = ((s8[25165824]{0:T(1024)(128)(4,1)}), s8[4194304]{0:T(1024)(128)(4,1)S(1)}, s32[]{:S(2)}) async-start(s8[25165824]{0:T(1024)(128)(4,1)} %bitcast.191), calls=%async_computation.15 | async-start | bytes 8388608
  257.8 1.7 copy-start.22
  259.4 4.1 slice-start.4
  260.6 3.2 slice-start.5
  261.0 2.8 copy-start.26
  261.0 2.8 copy-start.28
  273.2 4.4 copy-start.17
  277.6 13.6 %copy-start.4 = (pred[512,1024]{1,0:T(8,128)(4,1)S(1)}, pred[512,1024]{1,0:T(8,128)(4,1)}, u32[]{:S(2)}) copy-start(pred[512,1024]{1,0:T(8,128)(4,1)} %get-tuple-element.124) | copy-start | bytes 1572868
  277.6 13.6 %copy-start.16 = (bf16[512,768]{0,1:T(8,128)(2,1)S(1)}, bf16[512,768]{0,1:T(8,128)(2,1)}, u32[]{:S(2)}) copy-start(bf16[512,768]{0,1:T(8,128)(2,1)} %get-tuple-element.110) | copy-start | bytes 2359300
  277.6 13.6 %copy-start.24 = (f32[12,512]{1,0:T(8,128)S(1)}, f32[12,512]{1,0:T(8,128)}, u32[]{:S(2)}) copy-start(f32[12,512]{1,0:T(8,128)} %copy-done.23) | copy-start | bytes 73732
  291.2 13.5 %copy-start.9 = (bf16[1,1024,1,12,64]{1,4,3,2,0:T(8,128)(2,1)S(1)}, bf16[1,1024,1,12,64]{1,4,3,2,0:T(8,128)(2,1)}, u32[]{:S(2)}) copy-start(bf16[1,1024,1,12,64]{1,4,3,2,0:T(8,128)(2,1)} %maximum_bitcast_fusion.1) | copy-start | bytes 4718596
  291.2 146.6 %reduce-scatter.5.cloned.1.call-start = ((), (), s32[]{:S(2)}) async-start(), calls=%async_computation.8 | async-start | bytes 4423680 | tf_op jit(solution)/shard_map/reduce_scatter | solution.py:295
  291.3 13.4 %copy-start.10 = (bf16[1,1024,1,12,64]{1,4,3,2,0:T(8,128)(2,1)S(1)}, bf16[1,1024,1,12,64]{1,4,3,2,0:T(8,128)(2,1)}, u32[]{:S(2)}) copy-start(bf16[1,1024,1,12,64]{1,4,3,2,0:T(8,128)(2,1)} %maximum_bitcast_fusion.2) | copy-start | bytes 4718596
  304.7 3.1 copy-start.1
  304.7 3.1 copy-start.31
  304.7 3.0 copy-start.33
  304.7 3.0 copy-start.35
  304.7 3.0 copy-start.39
  305.6 2.2 copy-start.12
  313.8 124.0 %reduce-scatter.9.cloned.1.call-start = ((), (), s32[]{:S(2)}) async-start(), calls=%async_computation.10 | async-start | bytes 5898240 | tf_op jit(solution)/shard_map/reduce_scatter | solution.py:313
  314.5 37.4 %copy-start.8 = (bf16[1,1024,768]{2,1,0:T(8,128)(2,1)S(1)}, bf16[1,1024,768]{2,1,0:T(8,128)(2,1)}, u32[]{:S(2)}) copy-start(bf16[1,1024,768]{2,1,0:T(8,128)(2,1)} %param.17) | copy-start | bytes 4718596
  363.7 2.6 copy-start.53
  374.0 99.4 %reduce-scatter.11.cloned.1.call-start = ((), (), s32[]{:S(2)}) async-start(), calls=%async_computation.11 | async-start | bytes 5898240 | tf_op jit(solution)/shard_map/reduce_scatter | solution.py:319
  384.0 2.3 copy-start.51
  384.0 2.5 copy-start.52
  389.6 8.7 %copy-start.45 = (bf16[768,2304]{1,0:T(8,128)(2,1)S(1)}, bf16[768,2304]{1,0:T(8,128)(2,1)}, u32[]{:S(2)}) copy-start(bf16[768,2304]{1,0:T(8,128)(2,1)} %all-gather.6.cloned.1.call-done) | copy-start | bytes 10616836
  398.3 10.7 %copy-start.13 = (f32[1024,768]{1,0:T(8,128)}, f32[1024,768]{1,0:T(8,128)S(1)}, u32[]{:S(2)}) copy-start(f32[1024,768]{1,0:T(8,128)S(1)} %fusion.139) | copy-start | bytes 9437188
  421.9 8.8 %copy-start.18 = (bf16[1024,12,64]{0,2,1:T(8,128)(2,1)S(1)}, bf16[1024,12,64]{0,2,1:T(8,128)(2,1)}, u32[]{:S(2)}) copy-start(bf16[1024,12,64]{0,2,1:T(8,128)(2,1)} %pad_maximum_fusion.1) | copy-start | bytes 4718596
  421.9 8.8 %copy-start.46 = (bf16[768,768]{1,0:T(8,128)(2,1)S(1)}, bf16[768,768]{1,0:T(8,128)(2,1)}, u32[]{:S(2)}) copy-start(bf16[768,768]{1,0:T(8,128)(2,1)} %all-gather.8.cloned.1.call-done) | copy-start | bytes 3538948
  430.7 3.7 copy-start.14
  430.7 3.9 copy-start.15
  (7 other events, 5.4 us)
Sparse Core Ops, SparseCore 0:
  9.7 20.2 all-gather.7
  31.6 30.7 all-gather.5
  63.9 37.4 all-gather.9
  102.8 37.4 all-gather.11
  291.3 26.0 reduce-scatter.6
  320.0 40.3 reduce-scatter.4
  374.1 48.7 reduce-scatter.8
  425.6 47.7 reduce-scatter.10
where the time goes:
time: 764 us; the launch traced here: 760 us
  blocking collectives  310 us (41%)
  matrix products  262 us (34%)
  other arithmetic  83.3 us (11%)
  waiting for transfers between devices  58.3 us (8%)
  local copies, waits for them, and re-layouts  27.3 us (4%)
  between operations  18.6 us (2%)
    psum x1, blocking collectives, per_device(): lax.psum((owned[0], owned[1], owned[2], owned[3], owned[4], owned[5], own...  279 us
    convert_element_type x1, other arithmetic, attend_back(): (probabilities * (grad_probs - inner_sum)).astype(jnp.bfloat16)  42.1 us
    dot_general x1, matrix products, per_device(): jnp.dot(normed_two, full_up, preferred_element_type=jnp.float32)  37.4 us
    dot_general x2, matrix products, attend_back(): jnp.einsum('qhd,khd->hqk', grad_block, value_seq, preferred_element_type=...  37.3 us
    reduce_scatter x1, waiting for transfers between devices, per_device(): lax.psum_scatter(gradients[10].astype(jnp.bfloat16), 'shard', scatter_dim...  35.6 us
    dot_general x2, matrix products, attend_back(): jnp.einsum('hqk,qhd->khd', probabilities.astype(jnp.bfloat16), grad_block...  26.9 us
    unnamed x2, blocking collectives  25.4 us
    reduce_sum x2, other arithmetic, attend_sequence(): row_total = jnp.sum(exponent, -1, keepdims=True)  24.2 us
  transfers between devices with their start and end apart: 8, of which 2 were waited for; matrix products, arithmetic and copies ran while one was open for 48% of the time, Pallas kernels for 0%

commit v1 on v0

v1 whole, which is shorter than its diff:
```python
import functools
import math

import jax
import jax.numpy as jnp
from jax import lax
from jax.experimental import pallas as pl
from jax.experimental.pallas import tpu as pltpu
from jax.sharding import PartitionSpec as P

HEADS = 12
HEAD = 64
ROT = 16
PAIR = 2 * HEAD
SPAN = 512
BLOCK = 256

EPS = 1e-05
MASKED = -1e30
ROTARY_BASE = 10000.0

f32 = jnp.float32
bf16 = jnp.bfloat16


def swap(value, axis, size, bit):
    return lax.ppermute(value, axis, [(i, i ^ bit) for i in range(size)])


def bits_of(size):
    bits = []
    bit = 1
    while bit < size:
        bits.append(bit)
        bit *= 2
    return bits


def take(blocks, index):
    return lax.dynamic_index_in_dim(blocks, index, 0, keepdims=False)


def gather_rows(rows, shards):
    me = lax.axis_index("shard")
    blocks = rows[None]
    for bit in reversed(bits_of(shards)):
        other = swap(blocks, "shard", shards, bit)
        high = (me // bit) % 2 == 1
        first = jnp.where(high, other, blocks)
        second = jnp.where(high, blocks, other)
        blocks = jnp.stack([first, second], 0)
        blocks = blocks.reshape((-1,) + rows.shape) if bit == shards // 2 else blocks
        if bit != shards // 2:
            blocks = jnp.swapaxes(blocks, 0, 1).reshape((-1,) + rows.shape)
    return blocks.reshape((shards * rows.shape[0],) + rows.shape[1:])


def reduce_rows(grad, shards, replicas):
    me = lax.axis_index("shard")
    rep = lax.axis_index("replica")
    width = grad.shape[1]
    blocks = grad.astype(bf16).reshape(shards, -1, width)
    for bit in bits_of(shards):
        mine = (me // bit) % 2
        pairs = blocks.reshape((-1, 2) + blocks.shape[1:])
        kept = lax.dynamic_index_in_dim(pairs, mine, 1, keepdims=False)
        sent = lax.dynamic_index_in_dim(pairs, 1 - mine, 1, keepdims=False)
        other = swap(sent, "shard", shards, bit)
        blocks = (kept.astype(f32) + other.astype(f32)).astype(bf16)
    part = blocks[0]
    for bit in bits_of(replicas):
        mine = (rep // bit) % 2
        halves = part.reshape(2, -1, width)
        other = swap(take(halves, 1 - mine), "replica", replicas, bit)
        part = (take(halves, mine).astype(f32) + other.astype(f32)).astype(bf16)
    for bit in reversed(bits_of(replicas)):
        high = (rep // bit) % 2 == 1
        other = swap(part, "replica", replicas, bit)
        part = jnp.concatenate(
            [jnp.where(high, other, part), jnp.where(high, part, other)], 0
        )
    return part.astype(f32)


def total_vectors(vectors, shards, replicas):
    me = lax.axis_index("shard")
    packed = jnp.concatenate(vectors)[None]
    for bit in bits_of(shards):
        packed = packed + swap(packed, "shard", shards, bit)
    for bit in bits_of(replicas):
        packed = packed + swap(packed, "replica", replicas, bit)
    owned = []
    offset = 0
    for vector in vectors:
        size = vector.shape[0] // shards
        owned.append(lax.dynamic_slice(packed[0], (offset + me * size,), (size,)))
        offset += vector.shape[0]
    return owned


def dot(a, b, a_dim, b_dim):
    return lax.dot_general(a, b, (((a_dim,), (b_dim,)), ((), ())), preferred_element_type=f32)


def attention_kernel(
    q_ref, k_ref, v_ref, g_ref, cos_ref, low_ref, high_ref, start_ref,
    ctx_ref, dq_ref, dk_ref, dv_ref,
    q_s, k_s, v_s, dk_s, dv_s,
):
    length = q_ref.shape[0]
    cosine, low, high = cos_ref[...], low_ref[...], high_ref[...]

    def turned(u):
        return u * cosine + pltpu.roll(u, PAIR - ROT // 2, 1) * low + pltpu.roll(u, ROT // 2, 1) * high

    def back(rows, d):
        c, lo, hi = cos_ref[rows, :], low_ref[rows, :], high_ref[rows, :]
        return d * c - pltpu.roll(d, PAIR - ROT // 2, 1) * lo - pltpu.roll(d, ROT // 2, 1) * hi

    lane = lax.broadcasted_iota(jnp.int32, (1, PAIR), 1)
    heads = [lane < HEAD, lane >= HEAD]
    q_s[...] = (turned(q_ref[...]).astype(bf16).astype(f32) * HEAD ** (-0.5)).astype(bf16)
    k_s[...] = turned(k_ref[...]).astype(bf16)
    v_s[...] = v_ref[...].astype(bf16)
    dk_s[...] = jnp.zeros_like(dk_s)
    dv_s[...] = jnp.zeros_like(dv_s)

    def only(value, head):
        return jnp.where(head, value, jnp.zeros_like(value))

    for q0 in range(0, length, BLOCK):
        k0 = max(0, q0 - SPAN)
        count = q0 + BLOCK - k0
        rows = pl.ds(q0, BLOCK)
        keys = pl.ds(k0, count)
        q_block, g_block = q_s[rows, :], g_ref[rows, :]
        k_band, v_band = k_s[keys, :], v_s[keys, :]
        key_index = k0 + lax.broadcasted_iota(jnp.int32, (count, BLOCK), 0)
        query_index = q0 + lax.broadcasted_iota(jnp.int32, (count, BLOCK), 1)
        allowed = (key_index >= start_ref[:, rows]) & (key_index <= query_index)
        context = None
        for head in heads:
            q_head, g_head = only(q_block, head), only(g_block, head)
            scores = jnp.where(allowed, dot(k_band, q_head, 1, 1), MASKED)
            exponent = jnp.exp(scores - jnp.max(scores, 0, keepdims=True))
            probs = exponent * (1.0 / jnp.sum(exponent, 0, keepdims=True))
            probs_low = probs.astype(bf16)
            grad_probs = dot(v_band, g_head, 1, 1)
            product = probs * grad_probs
            inner = jnp.sum(product, 0, keepdims=True)
            grad_scores = (product - probs * inner).astype(bf16)
            ctx_part = dot(probs_low, only(v_band, head), 0, 0)
            dq_part = dot(grad_scores, only(k_band, head), 0, 0)
            context = ctx_part if context is None else context + ctx_part
            grad_q = dq_part if head is heads[0] else grad_q + dq_part
            dv_s[keys, :] += dot(probs_low, g_head, 1, 0)
            dk_s[keys, :] += dot(grad_scores, q_head, 1, 0)
        ctx_ref[rows, :] = context.astype(bf16)
        dq_ref[rows, :] = back(rows, grad_q * HEAD ** (-0.5)).astype(bf16)
    dk_ref[...] = back(slice(None), dk_s[...]).astype(bf16)
    dv_ref[...] = dv_s[...].astype(bf16)


def attention(qkv, grad_context, cosine, low, high, start):
    length, width = grad_context.shape
    pairs = width // PAIR
    block = lambda shift: pl.BlockSpec((length, PAIR), lambda i: (0, i + shift))
    table = pl.BlockSpec((length, PAIR), lambda i: (0, 0))
    out = jax.ShapeDtypeStruct((length, width), bf16)
    return pl.pallas_call(
        attention_kernel,
        grid=(pairs,),
        in_specs=[
            block(0), block(pairs), block(2 * pairs), block(0), table, table, table,
            pl.BlockSpec((1, length), lambda i: (0, 0)),
        ],
        out_specs=[block(0)] * 4,
        out_shape=[out] * 4,
        scratch_shapes=[pltpu.VMEM((length, PAIR), bf16)] * 3
        + [pltpu.VMEM((length, PAIR), f32)] * 2,
        compiler_params=pltpu.CompilerParams(vmem_limit_bytes=48 * 1024 * 1024),
        cost_estimate=pl.CostEstimate(
            flops=60_000_000_000, bytes_accessed=20_000_000, transcendentals=8_000_000
        ),
    )(qkv, qkv, qkv, grad_context, cosine, low, high, start)


def norm_back(cotangent, normal, inv_scale, gain):
    scaled = cotangent * gain
    first_term = jnp.mean(scaled, -1, keepdims=True)
    second_term = jnp.mean(scaled * normal, -1, keepdims=True)
    return inv_scale * (scaled - first_term - normal * second_term)


def rotary_tables(places):
    half = ROT // 2
    frequency = ROTARY_BASE ** (-(jnp.arange(half, dtype=f32) * 2.0 / ROT))
    angles = places.astype(f32)[:, None] * jnp.tile(frequency, PAIR // half)[None]
    lane = lax.broadcasted_iota(jnp.int32, angles.shape, 1) % HEAD
    sine = jnp.sin(angles)
    cosine = jnp.where(lane < ROT, jnp.cos(angles), 1.0)
    low = jnp.where(lane < half, -sine, 0.0)
    high = jnp.where((lane >= half) & (lane < ROT), sine, 0.0)
    return cosine, low, high


def matmul(a, b):
    return jnp.dot(a, b, preferred_element_type=f32)


def per_device(
    shards, replicas,
    tokens, segments, out_grad,
    ln1_gain, ln1_bias, w_qkv, b_qkv, w_attn, b_attn,
    ln2_gain, ln2_bias, w_up, b_up, w_down, b_down,
):
    _, length, width = tokens.shape
    vectors = [ln1_gain, ln1_bias, b_qkv, b_attn, ln2_gain, ln2_bias, b_up, b_down]
    packed = gather_rows(jnp.concatenate(vectors)[None], shards)
    full = []
    offset = 0
    for vector in vectors:
        size = vector.shape[0]
        full.append(packed[:, offset : offset + size].reshape(-1).astype(f32))
        offset += size
    gain_one, bias_one, bias_qkv, bias_attn, gain_two, bias_two, bias_up, bias_down = full
    full_up = gather_rows(w_up, shards)
    full_down = gather_rows(w_down, shards)
    full_qkv = gather_rows(w_qkv, shards)
    full_attn = gather_rows(w_attn, shards)

    grad_rows = out_grad.reshape(length, width)
    grad_float = grad_rows.astype(f32)
    inputs = tokens.reshape(length, width).astype(f32)
    centered = inputs - jnp.mean(inputs, -1, keepdims=True)
    inv_scale = lax.rsqrt(jnp.mean(centered * centered, -1, keepdims=True) + EPS)
    normal = centered * inv_scale
    normed_one = (normal * gain_one + bias_one).astype(bf16)
    normed_two = (normal * gain_two + bias_two).astype(bf16)

    hidden = matmul(normed_two, full_up) + bias_up
    cdf = 0.5 * (1.0 + lax.erf(hidden * (1.0 / math.sqrt(2.0))))
    activated = (hidden * cdf).astype(bf16)
    grad_w_down = dot(activated, grad_rows, 0, 0)
    out_down = reduce_rows(grad_w_down, shards, replicas)
    density = jnp.exp(-0.5 * hidden * hidden) * (1.0 / math.sqrt(2.0 * math.pi))
    slope = cdf + hidden * density
    grad_hidden = (dot(grad_rows, full_down, 1, 1) * slope).astype(bf16)
    grad_w_up = dot(normed_two, grad_hidden, 0, 0)
    out_up = reduce_rows(grad_w_up, shards, replicas)
    mlp_out = matmul(activated, full_down) + bias_down
    grad_normed_two = dot(grad_hidden, full_up, 1, 1)

    seg = segments.reshape(length)
    start = jnp.sum((seg[None, :] < seg[:, None]).astype(jnp.int32), 1)
    places = lax.iota(jnp.int32, length) - start
    cosine, low, high = rotary_tables(places)
    qkv = matmul(normed_one, full_qkv) + bias_qkv
    grad_context = dot(grad_rows, full_attn, 1, 1).astype(bf16)
    context, dq, dk, dv = attention(qkv, grad_context, cosine, low, high, start[None])
    grad_qkv = jnp.concatenate([dq, dk, dv], 1)
    grad_w_qkv = dot(normed_one, grad_qkv, 0, 0)
    out_qkv = reduce_rows(grad_w_qkv, shards, replicas)
    grad_w_attn = dot(context, grad_rows, 0, 0)
    out_attn = reduce_rows(grad_w_attn, shards, replicas)
    grad_normed_one = dot(grad_qkv, full_qkv, 1, 1)

    mixed = inputs + (matmul(context, full_attn) + bias_attn) + mlp_out
    tokens_grad = (
        grad_float
        + norm_back(grad_normed_one, normal, inv_scale, gain_one)
        + norm_back(grad_normed_two, normal, inv_scale, gain_two)
    )
    sums = total_vectors(
        [
            jnp.sum(grad_normed_one * normal, 0),
            jnp.sum(grad_normed_one, 0),
            jnp.sum(grad_qkv.astype(f32), 0),
            jnp.sum(grad_float, 0),
            jnp.sum(grad_normed_two * normal, 0),
            jnp.sum(grad_normed_two, 0),
            jnp.sum(grad_hidden.astype(f32), 0),
        ],
        shards,
        replicas,
    )
    g_gain_one, g_bias_one, g_b_qkv, g_b_attn, g_gain_two, g_bias_two, g_b_up = sums
    return (
        mixed[None], tokens_grad[None],
        g_gain_one, g_bias_one, out_qkv, g_b_qkv, out_attn, g_b_attn,
        g_gain_two, g_bias_two, out_up, g_b_up, out_down, g_b_attn,
    )


def solution(mesh):
    rows = P(("replica", "shard"), None, None)
    vec = P("shard")
    mat = P("shard", None)
    in_specs = (
        rows, P(("replica", "shard"), None), rows,
        vec, vec, mat, vec, mat, vec, vec, vec, mat, vec, mat, vec,
    )
    out_specs = (rows, rows, vec, vec, mat, vec, mat, vec, vec, vec, mat, vec, mat, vec)
    body = functools.partial(per_device, mesh.shape["shard"], mesh.shape["replica"])
    return jax.shard_map(body, mesh=mesh, in_specs=in_specs, out_specs=out_specs, check_vma=False)
```

time: 764 us -> 400 us (0.52)
  blocking collectives: 310 us -> 0 us
  matrix products: 262 us -> 82.1 us
  waiting for transfers between devices: 58.3 us -> 161 us
  starting transfers between devices: 0.32 us -> 48 us
  other arithmetic: 83.3 us -> 37.1 us
  Pallas kernels: 0 us -> 44.2 us
  between operations: 18.6 us -> 2.36 us
  local copies, waits for them, and re-layouts: 27.3 us -> 17.6 us
    psum x1 -> x0, blocking collectives: 279 us -> none  [per_device(): lax.psum((owned[0], owned[1], owned[2], owned[3], owned[4], owned[5], own...]
    dot_general x24 -> x12, matrix products: 262 us -> 82.1 us  [the longest x8 51.6 us: dot(): lax.dot_general(a, b, (((a_dim,), (b_dim,)), ((), ())), preferred_element...]
    ppermute x0 -> x47, waiting for transfers between devices: none -> 161 us  [swap(): return lax.ppermute(value, axis, [(i, i ^ bit) for i in range(size)])]
    ppermute x0 -> x47, starting transfers between devices: none -> 48 us  [swap(): return lax.ppermute(value, axis, [(i, i ^ bit) for i in range(size)])]
    pallas_call x0 -> x1, Pallas kernels: none -> 44.2 us  [attention(): pl.pallas_call(attention_kernel, grid=(pairs,), in_specs=[block(0), block...]
    reduce_scatter x4 -> x0, waiting for transfers between devices: 35.6 us -> none  [the longest x1 35.6 us: per_device(): lax.psum_scatter(gradients[10].astype(jnp.bfloat16), 'shard', scatter_dim...]
    convert_element_type x17 -> x28, other arithmetic: 44.5 us -> 11 us  [the longest x4 5.42 us: reduce_rows(): return part.astype(f32)]
    unnamed x2 -> x0, blocking collectives: 25.4 us -> none
  transfers between devices with their start and end apart: 8 -> 47, of which waited for: 2 -> 25; matrix products, arithmetic and copies ran while one was open for 48% -> 33% of each run, Pallas kernels for 0% -> 11%
where the time goes in v1:
time: 400 us; the launch traced here: 393 us
  waiting for transfers between devices  161 us (40%)
  matrix products  82.1 us (21%)
  starting transfers between devices  48 us (12%)
  Pallas kernels  44.2 us (11%)
  other arithmetic  37.1 us (9%)
  local copies, waits for them, and re-layouts  17.6 us (4%)
    ppermute x47, waiting for transfers between devices, swap(): return lax.ppermute(value, axis, [(i, i ^ bit) for i in range(size)])  161 us
    dot_general x8, matrix products, dot(): lax.dot_general(a, b, (((a_dim,), (b_dim,)), ((), ())), preferred_element...  51.6 us
    ppermute x47, starting transfers between devices, swap(): return lax.ppermute(value, axis, [(i, i ^ bit) for i in range(size)])  48 us
    pallas_call x1, Pallas kernels, attention(): pl.pallas_call(attention_kernel, grid=(pairs,), in_specs=[block(0), block...  44.2 us
    dot_general x4, matrix products, matmul(): return jnp.dot(a, b, preferred_element_type=f32)  30.5 us
    another operation x14, other arithmetic, gather_rows(): blocks = jnp.stack([first, second], 0)  10.8 us
  transfers between devices with their start and end apart: 47, of which 25 were waited for; matrix products, arithmetic and copies ran while one was open for 33% of the time, Pallas kernels for 11%

profile of v1, /device:TPU:0, one launch (start us, length us, event | category | flops | bytes accessed | tf_op | source)
XLA Modules:
  0.0 392.9 jit_solution(1323456047494935287)
XLA Ops:
  0.7 3.0 collective-permute-start.2
  3.7 5.4 %concatenate.45 = bf16[2496]{0:T(1024)(128)(2,1)S(1)} concatenate(bf16[192]{0:T(256)(128)(2,1)} %param.18, bf16[192]{0:T(256)(128)(2,1)} %param.19, bf16[576]{0:T(1024)(128)(2,1)} %param.21, bf16[192]{0:T(256)(128)(2,1)} %param.23, bf16[192]{0:T(256)(128)(2,1)} %param.24, bf16[192]{0:T(256)(128)(2,1)} %param.25, bf16[768]{0:T(1024)(128)(2,1)} %param.27, bf16[192]{0:T(256)(128)(2,1)} %param.29), dimensions={0} | concatenate | bytes 9984 | tf_op jit(solution)/shard_map/concatenate | solution.py:219
  9.3 1.9 collective-permute-start.4
  11.4 1.9 collective-permute-start.8
  13.3 1.7 convert_reduce_fusion.2
  16.4 2.0 fusion.83
  19.1 5.5 %collective-permute-done = bf16[1,1,2496]{2,1,0:T(2,128)(2,1)S(1)} collective-permute-done((bf16[1,1,2496]{2,1,0:T(2,128)(2,1)S(1)}, bf16[1,1,2496]{2,1,0:T(2,128)(2,1)S(1)}, u32[]{:S(2)}, u32[]{:S(2)}) %collective-permute-start) | collective-permute-done | bytes 5024 | tf_op jit(solution)/shard_map/ppermute | solution.py:27
  29.6 1.4 collective-permute-done.4
  35.1 2.6 fusion.76.g_ref
  37.7 18.7 %collective-permute-done.6 = bf16[1,192,3072]{2,1,0:T(8,128)(2,1)} collective-permute-done((bf16[1,192,3072]{2,1,0:T(8,128)(2,1)}, bf16[1,192,3072]{2,1,0:T(8,128)(2,1)}, u32[]{:S(2)}, u32[]{:S(2)}) %collective-permute-start.6) | collective-permute-done | bytes 1179680 | tf_op jit(solution)/shard_map/ppermute | solution.py:27
  56.3 1.4 select_bitcast_fusion.9
  57.8 1.6 maximum_bitcast_fusion
  59.4 21.4 %collective-permute-done.8 = bf16[1,768,768]{2,1,0:T(8,128)(2,1)} collective-permute-done((bf16[1,768,768]{2,1,0:T(8,128)(2,1)}, bf16[1,768,768]{2,1,0:T(8,128)(2,1)}, u32[]{:S(2)}, u32[]{:S(2)}) %collective-permute-start.8) | collective-permute-done | bytes 1179680 | tf_op jit(solution)/shard_map/ppermute | solution.py:27
  80.8 1.4 select_bitcast_fusion.7
  82.2 1.6 maximum_bitcast_fusion.1
  84.4 7.1 %convolution_add_fusion.q_ref.k_ref.v_ref = f32[1024,2304]{1,0:T(8,128)} fusion(bf16[768,2304]{1,0:T(8,128)(2,1)S(1)} %bitcast.344, f32[2304]{0:T(1024)S(1)} %reshape.316, bf16[1,1024,768]{2,1,0:T(8,128)(2,1)S(1)} %copy-done, f32[768]{0:T(1024)S(1)} %reshape.315, f32[768]{0:T(1024)S(1)} %reshape.314, f32[1024]{0:T(1024)S(1)} %add_rsqrt_fusion, ...), kind=kOutput, calls=%fused_computation.11 | convolution fusion | flops 3630956544 | bytes 14572544 | tf_op jit(solution)/shard_map/dot_general | solution.py:208
  91.5 44.2 %shard_map.254 = (bf16[1024,768]{1,0:T(8,128)(2,1)S(1)}, bf16[1024,768]{1,0:T(8,128)(2,1)S(1)}, bf16[1024,768]{1,0:T(8,128)(2,1)}, bf16[1024,768]{1,0:T(8,128)(2,1)}) custom-call(f32[1024,2304]{1,0:T(8,128)} %convolution_add_fusion.q_ref.k_ref.v_ref, f32[1024,2304]{1,0:T(8,128)} %convolution_add_fusion.q_ref.k_ref.v_ref, ...), custom_call_target="tpu_custom_call" | custom-call | flops 60000002048 | bytes 20000000 | tf_op jit(solution)/shard_map/pallas_call | solution.py:170
  137.8 4.6 %convolution_convert_fusion.2 = bf16[768,2304]{1,0:T(8,128)(2,1)S(1)} fusion(bf16[1024,2304]{1,0:T(8,128)(2,1)S(1)} %constant_dynamic-update-slice_fusion, bf16[1,1024,768]{2,1,0:T(8,128)(2,1)S(1)} %copy-done, f32[768]{0:T(1024)S(1)} %reshape.315, f32[768]{0:T(1024)S(1)} %reshape.314, f32[1024]{0:T(1024)S(1)} %add_rsqrt_fusion, ...), kind=kOutput, calls=%fused_computation.14 | convolution fusion | flops 3630366720 | bytes 9844736 | tf_op jit(solution)/shard_map/dot_general | solution.py:102
  142.4 1.3 dynamic-slice_bitcast_fusion.2
  144.9 1.4 fusion.73
  148.3 3.1 fusion.103
  151.6 1.8 collective-permute-start.24
  153.4 2.0 select_bitcast_fusion.3
  155.8 2.0 select_bitcast_fusion.1
  158.5 11.7 %multiply_convert_fusion = (bf16[1024,3072]{1,0:T(8,128)(2,1)}, f32[1024,3072]{1,0:T(8,128)}) fusion(f32[3072]{0:T(1024)S(1)} %copy-done.24, bf16[768,3072]{1,0:T(8,128)(2,1)S(1)} %bitcast.338, bf16[1,1024,768]{2,1,0:T(8,128)(2,1)S(1)} %copy-done, f32[768]{0:T(1024)S(1)} %copy-done.28, f32[768]{0:T(1024)S(1)} %copy-done.23, f32[1024]{0:T(1024)S(1)} %copy-done.20, ...), kind=kOutput, calls=%fused_computation.8 | convolution fusion | flops 4855431168 | bytes 25192448 | tf_op jit(solution)/shard_map/dot_general | solution.py:208
  170.2 13.4 %convert_reduce_fusion = (f32[3072]{0:T(1024)S(1)}, bf16[1024,3072]{1,0:T(8,128)(2,1)}) fusion(f32[1024,3072]{1,0:T(8,128)} %get-tuple-element.95, f32[3072]{0:T(1024)S(1)} %copy-done.24, bf16[3072,768]{1,0:T(8,128)(2,1)S(1)} %bitcast.336, bf16[1,1024,768]{2,1,0:T(8,128)(2,1)S(1)} %copy-done.8), kind=kOutput, calls=%fused_computation.7 | convolution fusion | flops 4872729600 | bytes 25190400 | tf_op jit(solution)/shard_map/dot_general | solution.py:102
  183.6 7.3 %fusion.104 = f32[1024,768]{1,0:T(8,128)S(1)} fusion(bf16[1024,3072]{1,0:T(8,128)(2,1)} %get-tuple-element.98, bf16[768,3072]{1,0:T(8,128)(2,1)S(1)} %bitcast.339), kind=kOutput, calls=%fused_computation.261 | convolution fusion | flops 4831838208 | bytes 14155776 | tf_op jit(solution)/shard_map/dot_general | solution.py:102
  191.0 8.9 %convolution_convert_fusion.1 = bf16[768,3072]{1,0:T(8,128)(2,1)S(1)} fusion(bf16[1024,3072]{1,0:T(8,128)(2,1)} %get-tuple-element.98, bf16[1,1024,768]{2,1,0:T(8,128)(2,1)S(1)} %copy-done, f32[768]{0:T(1024)S(1)} %copy-done.28, f32[768]{0:T(1024)S(1)} %copy-done.23, f32[1024]{0:T(1024)S(1)} %copy-done.20, f32[1024]{0:T(1024)S(1)} %copy-done.17), kind=kOutput, calls=%fused_computation.13 | convolution fusion | flops 4838916096 | bytes 12597248 | tf_op jit(solution)/shard_map/dot_general | solution.py:102
  199.9 4.9 %fusion.29 = (f32[768]{0:T(1024)S(1)}, f32[1024]{0:T(1024)S(1)}, f32[1024]{0:T(1024)S(1)}, f32[768]{0:T(1024)S(1)}, f32[768]{0:T(1024)S(1)}, /*index=5*/f32[1024...) fusion(bf16[1,1024,768]{2,1,0:T(8,128)(2,1)S(1)} %copy-done, f32[1024]{0:T(1024)S(1)} %copy-done.20, ...), kind=kOutput, calls=%fused_computation.50 | convolution fusion | flops 3637240832 | bytes 16164864 | tf_op jit(solution)/shard_map/dot_general | solution.py:102
  204.9 3.4 convert_reduce_fusion.4
  208.6 1.6 collective-permute-start.25
  211.0 3.2 collective-permute-done.11
  215.4 1.6 collective-permute-start.26
  217.0 8.5 %convolution_convert_fusion = bf16[3072,768]{1,0:T(8,128)(2,1)S(1)} fusion(bf16[1024,3072]{1,0:T(8,128)(2,1)} %get-tuple-element.94, bf16[1,1024,768]{2,1,0:T(8,128)(2,1)S(1)} %copy-done.8), kind=kOutput, calls=%fused_computation.12 | convolution fusion | flops 4834197504 | bytes 12582912 | tf_op jit(solution)/shard_map/dot_general | solution.py:102
  226.2 2.7 collective-permute-start.27
  229.7 2.6 collective-permute-start.14
  232.4 1.6 collective-permute-start.28
  234.0 1.9 fusion.20
  236.5 8.7 %fusion.37 = f32[1,1024,768]{2,1,0:T(8,128)} fusion(bf16[1,1024,768]{2,1,0:T(8,128)(2,1)S(1)} %copy-done, f32[1024,768]{1,0:T(8,128)S(1)} %copy-done.29, bf16[1024,3072]{1,0:T(8,128)(2,1)} %get-tuple-element.94, bf16[3072,768]{1,0:T(8,128)(2,1)S(1)} %bitcast.337, f32[768]{0:T(1024)S(1)} %copy-done.26, f32[768]{0:T(1024)S(1)} %copy-done.27), kind=kOutput, calls=%fused_computation.58 | convolution fusion | flops 4835770368 | bytes 18880512 | tf_op jit(solution)/shard_map/dot_general | solution.py:208
  245.3 2.6 collective-permute-start.29
  247.8 8.0 %collective-permute-done.16 = bf16[1,192,2304]{2,1,0:T(8,128)(2,1)S(1)} collective-permute-done((bf16[1,192,2304]{2,1,0:T(8,128)(2,1)S(1)}, bf16[1,192,2304]{2,1,0:T(8,128)(2,1)S(1)}, u32[]{:S(2)}, u32[]{:S(2)}) %collective-permute-start.16) | collective-permute-done | bytes 884768 | tf_op jit(solution)/shard_map/ppermute | solution.py:27
  260.2 6.9 %collective-permute-done.17 = bf16[96,2304]{1,0:T(8,128)(2,1)S(1)} collective-permute-done((bf16[96,2304]{1,0:T(8,128)(2,1)S(1)}, bf16[96,2304]{1,0:T(8,128)(2,1)S(1)}, u32[]{:S(2)}, u32[]{:S(2)}) %collective-permute-start.17) | collective-permute-done | bytes 442400 | tf_op jit(solution)/shard_map/ppermute | solution.py:27
  269.6 4.8 %collective-permute-done.18 = bf16[48,2304]{1,0:T(8,128)(2,1)S(1)} collective-permute-done((bf16[48,2304]{1,0:T(8,128)(2,1)S(1)}, bf16[48,2304]{1,0:T(8,128)(2,1)S(1)}, u32[]{:S(2)}, u32[]{:S(2)}) %collective-permute-start.18) | collective-permute-done | bytes 221216 | tf_op jit(solution)/shard_map/ppermute | solution.py:27
  275.6 5.4 %collective-permute-done.19 = bf16[24,2304]{1,0:T(8,128)(2,1)S(1)} collective-permute-done((bf16[24,2304]{1,0:T(8,128)(2,1)S(1)}, bf16[24,2304]{1,0:T(8,128)(2,1)S(1)}, u32[]{:S(2)}, u32[]{:S(2)}) %collective-permute-start.19) | collective-permute-done | bytes 110624 | tf_op jit(solution)/shard_map/ppermute | solution.py:27
  281.8 5.2 %collective-permute-done.20 = bf16[24,2304]{1,0:T(8,128)(2,1)S(1)} collective-permute-done((bf16[24,2304]{1,0:T(8,128)(2,1)S(1)}, bf16[24,2304]{1,0:T(8,128)(2,1)S(1)}, u32[]{:S(2)}, u32[]{:S(2)}) %collective-permute-start.20) | collective-permute-done | bytes 110624 | tf_op jit(solution)/shard_map/ppermute | solution.py:27
  288.5 4.6 %collective-permute-done.21 = bf16[48,2304]{1,0:T(8,128)(2,1)S(1)} collective-permute-done((bf16[48,2304]{1,0:T(8,128)(2,1)S(1)}, bf16[48,2304]{1,0:T(8,128)(2,1)S(1)}, u32[]{:S(2)}, u32[]{:S(2)}) %collective-permute-start.21) | collective-permute-done | bytes 221216 | tf_op jit(solution)/shard_map/ppermute | solution.py:27
  294.0 16.2 %collective-permute-done.32 = bf16[1,192,3072]{2,1,0:T(8,128)(2,1)S(1)} collective-permute-done((bf16[1,192,3072]{2,1,0:T(8,128)(2,1)S(1)}, bf16[1,192,3072]{2,1,0:T(8,128)(2,1)S(1)}, u32[]{:S(2)}, u32[]{:S(2)}) %collective-permute-start.32) | collective-permute-done | bytes 1179680 | tf_op jit(solution)/shard_map/ppermute | solution.py:27
  311.9 14.5 %collective-permute-done.40 = bf16[1,768,768]{2,1,0:T(8,128)(2,1)S(1)} collective-permute-done((bf16[1,768,768]{2,1,0:T(8,128)(2,1)S(1)}, bf16[1,768,768]{2,1,0:T(8,128)(2,1)S(1)}, u32[]{:S(2)}, u32[]{:S(2)}) %collective-permute-start.40) | collective-permute-done | bytes 1179680 | tf_op jit(solution)/shard_map/ppermute | solution.py:27
  328.3 8.3 %collective-permute-done.41 = bf16[384,768]{1,0:T(8,128)(2,1)S(1)} collective-permute-done((bf16[384,768]{1,0:T(8,128)(2,1)S(1)}, bf16[384,768]{1,0:T(8,128)(2,1)S(1)}, u32[]{:S(2)}, u32[]{:S(2)}) %collective-permute-start.41) | collective-permute-done | bytes 589856 | tf_op jit(solution)/shard_map/ppermute | solution.py:27
  337.7 2.9 collective-permute-start.35
  340.6 5.9 %collective-permute-done.42 = bf16[192,768]{1,0:T(8,128)(2,1)S(1)} collective-permute-done((bf16[192,768]{1,0:T(8,128)(2,1)S(1)}, bf16[192,768]{1,0:T(8,128)(2,1)S(1)}, u32[]{:S(2)}, u32[]{:S(2)}) %collective-permute-start.42) | collective-permute-done | bytes 294944 | tf_op jit(solution)/shard_map/ppermute | solution.py:27
  346.7 1.8 collective-permute-start.43
  348.5 3.0 collective-permute-start.36
  351.4 4.2 %collective-permute-done.43 = bf16[96,768]{1,0:T(8,128)(2,1)S(1)} collective-permute-done((bf16[96,768]{1,0:T(8,128)(2,1)S(1)}, bf16[96,768]{1,0:T(8,128)(2,1)S(1)}, u32[]{:S(2)}, u32[]{:S(2)}) %collective-permute-start.43) | collective-permute-done | bytes 147488 | tf_op jit(solution)/shard_map/ppermute | solution.py:27
  355.8 3.1 collective-permute-done.36
  358.9 2.5 collective-permute-start.37
  362.0 2.6 collective-permute-start.45
  364.6 3.6 collective-permute-done.37
  368.5 1.3 maximum_convert_fusion.2
  369.8 1.6 collective-permute-done.45
  372.0 11.7 %collective-permute-done.38 = bf16[96,3072]{1,0:T(8,128)(2,1)S(1)} collective-permute-done((bf16[96,3072]{1,0:T(8,128)(2,1)S(1)}, bf16[96,3072]{1,0:T(8,128)(2,1)S(1)}, u32[]{:S(2)}, u32[]{:S(2)}) %collective-permute-start.38) | collective-permute-done | bytes 589856 | tf_op jit(solution)/shard_map/ppermute | solution.py:27
  384.0 1.7 maximum_convert_fusion
  385.6 4.4 %collective-permute-done.46 = bf16[384,768]{1,0:T(8,128)(2,1)S(1)} collective-permute-done((bf16[384,768]{1,0:T(8,128)(2,1)S(1)}, bf16[384,768]{1,0:T(8,128)(2,1)S(1)}, u32[]{:S(2)}, u32[]{:S(2)}) %collective-permute-start.46) | collective-permute-done | bytes 589856 | tf_op jit(solution)/shard_map/ppermute | solution.py:27
  390.3 1.6 maximum_convert_fusion.1
  (240 shorter events, 41.2 us)
Async XLA Ops:
  0.6 17.8 %copy-start = (bf16[1,1024,768]{2,1,0:T(8,128)(2,1)S(1)}, bf16[1,1024,768]{2,1,0:T(8,128)(2,1)}, u32[]{:S(2)}) copy-start(bf16[1,1024,768]{2,1,0:T(8,128)(2,1)} %param.15) | copy-start | bytes 4718596
  0.7 31.5 %collective-permute-start.2 = (bf16[1,192,2304]{2,1,0:T(8,128)(2,1)}, bf16[1,192,2304]{2,1,0:T(8,128)(2,1)}, u32[]{:S(2)}, u32[]{:S(2)}) collective-permute-start(bf16[1,192,2304]{2,1,0:T(8,128)(2,1)} %bitcast.370), channel_id=1, source_target_pairs={{0,2},{1,3},{2,0},{3,1},{4,6},{5,7},{6,4},{7,5},{8,10},{9,11},{10,... | collective-permute-start | bytes 2654216 | tf_op jit(solution)/shard_map/ppermute | solution.py:27
  9.1 15.5 %collective-permute-start = (bf16[1,1,2496]{2,1,0:T(2,128)(2,1)S(1)}, bf16[1,1,2496]{2,1,0:T(2,128)(2,1)S(1)}, u32[]{:S(2)}, u32[]{:S(2)}) collective-permute-start(bf16[1,1,2496]{2,1,0:T(2,128)(2,1)S(1)} %broadcast_in_dim_broadcast_in_dim.3), channel_id=1, source_target_pairs={{0,2},{1,3},{2,0},{3,1},{4,6},{5,7},{6,4},{7,5},{8,10},{9,11},{10,... | collective-permute-start | bytes 14984 | tf_op jit(solution)/shard_map/ppermute | solution.py:27
  9.3 21.7 %collective-permute-start.4 = (bf16[1,192,768]{2,1,0:T(8,128)(2,1)}, bf16[1,192,768]{2,1,0:T(8,128)(2,1)}, u32[]{:S(2)}, u32[]{:S(2)}) collective-permute-start(bf16[1,192,768]{2,1,0:T(8,128)(2,1)} %bitcast.375), channel_id=1, source_target_pairs={{0,2},{1,3},{2,0},{3,1},{4,6},{5,7},{6,4},{7,5},{8,10},{9,11},{10,... | collective-permute-start | bytes 884744 | tf_op jit(solution)/shard_map/ppermute | solution.py:27
  11.2 45.1 %collective-permute-start.6 = (bf16[1,192,3072]{2,1,0:T(8,128)(2,1)}, bf16[1,192,3072]{2,1,0:T(8,128)(2,1)}, u32[]{:S(2)}, u32[]{:S(2)}) collective-permute-start(bf16[1,192,3072]{2,1,0:T(8,128)(2,1)} %bitcast.356), channel_id=1, source_target_pairs={{0,2},{1,3},{2,0},{3,1},{4,6},{5,7},{6,4},{7,5},{8,10},{9,11},{10,... | collective-permute-start | bytes 3538952 | tf_op jit(solution)/shard_map/ppermute | solution.py:27
  11.4 69.4 %collective-permute-start.8 = (bf16[1,768,768]{2,1,0:T(8,128)(2,1)}, bf16[1,768,768]{2,1,0:T(8,128)(2,1)}, u32[]{:S(2)}, u32[]{:S(2)}) collective-permute-start(bf16[1,768,768]{2,1,0:T(8,128)(2,1)} %bitcast.357), channel_id=1, source_target_pairs={{0,2},{1,3},{2,0},{3,1},{4,6},{5,7},{6,4},{7,5},{8,10},{9,11},{10,... | collective-permute-start | bytes 3538952 | tf_op jit(solution)/shard_map/ppermute | solution.py:27
  15.0 16.1 %copy-start.14 = (bf16[192,768]{1,0:T(8,128)(2,1)S(1)}, bf16[192,768]{1,0:T(8,128)(2,1)}, u32[]{:S(2)}) copy-start(bf16[192,768]{1,0:T(8,128)(2,1)} %param.22) | copy-start | bytes 884740
  15.0 122.8 %copy-start.16 = (f32[1024]{0:T(1024)}, f32[1024]{0:T(1024)S(1)}, u32[]{:S(2)}) copy-start(f32[1024]{0:T(1024)S(1)} %broadcast_multiply_fusion.4) | copy-start | bytes 12292
  24.7 1.2 collective-permute-start.1
  24.8 113.0 %copy-start.19 = (f32[1024]{0:T(1024)}, f32[1024]{0:T(1024)S(1)}, u32[]{:S(2)}) copy-start(f32[1024]{0:T(1024)S(1)} %add_rsqrt_fusion) | copy-start | bytes 12292
  26.4 111.4 %copy-start.21 = (f32[768]{0:T(1024)}, f32[768]{0:T(1024)S(1)}, u32[]{:S(2)}) copy-start(f32[768]{0:T(1024)S(1)} %reshape.314) | copy-start | bytes 9220
  32.1 2.1 collective-permute-start.5
  33.7 50.1 %collective-permute-start.3 = (bf16[2,192,2304]{2,1,0:T(8,128)(2,1)S(1)}, bf16[2,192,2304]{2,1,0:T(8,128)(2,1)S(1)}, u32[]{:S(2)}, u32[]{:S(2)}) collective-permute-start(bf16[2,192,2304]{2,1,0:T(8,128)(2,1)S(1)} %maximum_bitcast_fusion.2), channel_id=1, source_target_pairs={{0,1},{1,0},{2,3},{3,2},{4,5},{5,4},{6,7},{7,6},{8,9},{9,8},{10,11... | collective-permute-start | bytes 5308424 | tf_op jit(solution)/shard_map/ppermute | solution.py:27
  35.1 21.2 %copy-start.9 = (bf16[192,3072]{1,0:T(8,128)(2,1)S(1)}, bf16[192,3072]{1,0:T(8,128)(2,1)}, u32[]{:S(2)}) copy-start(bf16[192,3072]{1,0:T(8,128)(2,1)} %param.26) | copy-start | bytes 3538948
  57.7 23.0 %copy-start.10 = (bf16[768,768]{1,0:T(8,128)(2,1)S(1)}, bf16[768,768]{1,0:T(8,128)(2,1)}, u32[]{:S(2)}) copy-start(bf16[768,768]{1,0:T(8,128)(2,1)} %param.28) | copy-start | bytes 3538948
  59.4 94.0 %collective-permute-start.7 = (bf16[2,192,3072]{2,1,0:T(8,128)(2,1)}, bf16[2,192,3072]{2,1,0:T(8,128)(2,1)}, u32[]{:S(2)}, u32[]{:S(2)}) collective-permute-start(bf16[2,192,3072]{2,1,0:T(8,128)(2,1)} %maximum_bitcast_fusion), channel_id=1, source_target_pairs={{0,1},{1,0},{2,3},{3,2},{4,5},{5,4},{6,7},{7,6},{8,9},{9,8},{10,11... | collective-permute-start | bytes 7077896 | tf_op jit(solution)/shard_map/ppermute | solution.py:27
  83.8 72.0 %collective-permute-start.9 = (bf16[2,768,768]{2,1,0:T(8,128)(2,1)}, bf16[2,768,768]{2,1,0:T(8,128)(2,1)}, u32[]{:S(2)}, u32[]{:S(2)}) collective-permute-start(bf16[2,768,768]{2,1,0:T(8,128)(2,1)} %maximum_bitcast_fusion.1), channel_id=1, source_target_pairs={{0,1},{1,0},{2,3},{3,2},{4,5},{5,4},{6,7},{7,6},{8,9},{9,8},{10,11... | collective-permute-start | bytes 7077896 | tf_op jit(solution)/shard_map/ppermute | solution.py:27
  84.4 7.2 %copy-start.1 = (bf16[2,2,192,2304]{3,2,0,1:T(8,128)(2,1)}, bf16[2,2,192,2304]{3,2,0,1:T(8,128)(2,1)S(1)}, u32[]{:S(2)}) copy-start(bf16[2,2,192,2304]{3,2,0,1:T(8,128)(2,1)S(1)} %pad_maximum_fusion.2) | copy-start | bytes 10616836
  143.7 90.3 %collective-permute-start.15 = (bf16[2,192,2304]{2,1,0:T(8,128)(2,1)}, bf16[2,192,2304]{2,1,0:T(8,128)(2,1)}, u32[]{:S(2)}, u32[]{:S(2)}) collective-permute-start(bf16[2,192,2304]{2,1,0:T(8,128)(2,1)} %dynamic-slice_bitcast_fusion.2), channel_id=1, source_target_pairs={{0,1},{1,0},{2,3},{3,2},{4,5},{5,4},{6,7},{7,6},{8,9},{9,8},{10,11... | collective-permute-start | bytes 5308424 | tf_op jit(solution)/shard_map/ppermute | solution.py:27
  146.4 4.9 %collective-permute-start.23 = (bf16[2,192,768]{2,1,0:T(8,128)(2,1)S(1)}, bf16[2,192,768]{2,1,0:T(8,128)(2,1)S(1)}, u32[]{:S(2)}, u32[]{:S(2)}) collective-permute-start(bf16[2,192,768]{2,1,0:T(8,128)(2,1)S(1)} %dynamic-slice_bitcast_fusion.5), channel_id=1, source_target_pairs={{0,1},{1,0},{2,3},{3,2},{4,5},{5,4},{6,7},{7,6},{8,9},{9,8},{10,11... | collective-permute-start | bytes 1769480 | tf_op jit(solution)/shard_map/ppermute | solution.py:27
  151.6 56.9 %collective-permute-start.24 = (bf16[1,192,768]{2,1,0:T(8,128)(2,1)S(1)}, bf16[1,192,768]{2,1,0:T(8,128)(2,1)S(1)}, u32[]{:S(2)}, u32[]{:S(2)}) collective-permute-start(bf16[1,192,768]{2,1,0:T(8,128)(2,1)S(1)} %constant_dynamic-slice_fusion.6), channel_id=1, source_target_pairs={{0,2},{1,3},{2,0},{3,1},{4,6},{5,7},{6,4},{7,5},{8,10},{9,11},{10,... | collective-permute-start | bytes 884744 | tf_op jit(solution)/shard_map/ppermute | solution.py:27
  190.9 8.9 %copy-start.2 = (bf16[2,2,192,2304]{3,2,0,1:T(8,128)(2,1)S(1)}, bf16[2,2,192,2304]{3,2,0,1:T(8,128)(2,1)}, u32[]{:S(2)}) copy-start(bf16[2,2,192,2304]{3,2,0,1:T(8,128)(2,1)} %copy-done.1) | copy-start | bytes 10616836
  190.9 8.9 %copy-start.22 = (f32[768]{0:T(1024)S(1)}, f32[768]{0:T(1024)}, u32[]{:S(2)}) copy-start(f32[768]{0:T(1024)} %copy-done.21) | copy-start | bytes 9220
  199.8 5.0 %copy-start.18 = (f32[9216]{0:T(1024)S(1)}, f32[9216]{0:T(1024)}, u32[]{:S(2)}) copy-start(f32[9216]{0:T(1024)} %custom-call) | copy-start | bytes 110596
  199.8 5.0 %copy-start.15 = (f32[2304]{0:T(1024)S(1)}, f32[2304]{0:T(1024)}, u32[]{:S(2)}) copy-start(f32[2304]{0:T(1024)} %convert_reduce_fusion.1) | copy-start | bytes 27652
  208.4 1.8 collective-permute-start.10
  208.6 6.7 %collective-permute-start.25 = (bf16[96,768]{1,0:T(8,128)(2,1)S(1)}, bf16[96,768]{1,0:T(8,128)(2,1)S(1)}, u32[]{:S(2)}, u32[]{:S(2)}) collective-permute-start(bf16[96,768]{1,0:T(8,128)(2,1)S(1)} %dynamic-slice_bitcast_fusion.12), channel_id=1, source_target_pairs={{0,4},{4,0},{8,12},{12,8},{16,20},{20,16},{24,28},{28,24},{1,5},{5... | collective-permute-start | bytes 442376 | tf_op jit(solution)/shard_map/ppermute | solution.py:27
  210.2 4.0 %collective-permute-start.11 = (f32[1,9216]{1,0:T(1,128)S(1)}, f32[1,9216]{1,0:T(1,128)S(1)}, u32[]{:S(2)}, u32[]{:S(2)}) collective-permute-start(f32[1,9216]{1,0:T(1,128)S(1)} %add.378), channel_id=1, source_target_pairs={{0,2},{1,3},{2,0},{3,1},{4,6},{5,7},{6,4},{7,5},{8,10},{9,11},{10,... | collective-permute-start | bytes 110600 | tf_op jit(solution)/shard_map/ppermute | solution.py:27
  210.9 63.8 %collective-permute-start.31 = (bf16[2,192,3072]{2,1,0:T(8,128)(2,1)S(1)}, bf16[2,192,3072]{2,1,0:T(8,128)(2,1)S(1)}, u32[]{:S(2)}, u32[]{:S(2)}) collective-permute-start(bf16[2,192,3072]{2,1,0:T(8,128)(2,1)S(1)} %dynamic-slice_bitcast_fusion.1), channel_id=1, source_target_pairs={{0,1},{1,0},{2,3},{3,2},{4,5},{5,4},{6,7},{7,6},{8,9},{9,8},{10,11... | collective-permute-start | bytes 7077896 | tf_op jit(solution)/shard_map/ppermute | solution.py:27
  214.3 11.3 %collective-permute-start.12 = (f32[1,9216]{1,0:T(1,128)S(1)}, f32[1,9216]{1,0:T(1,128)S(1)}, u32[]{:S(2)}, u32[]{:S(2)}) collective-permute-start(f32[1,9216]{1,0:T(1,128)S(1)} %add.379), channel_id=1, source_target_pairs={{0,4},{4,0},{8,12},{12,8},{16,20},{20,16},{24,28},{28,24},{1,5},{5... | collective-permute-start | bytes 110600 | tf_op jit(solution)/shard_map/ppermute | solution.py:27
  215.4 10.7 %collective-permute-start.26 = (bf16[48,768]{1,0:T(8,128)(2,1)S(1)}, bf16[48,768]{1,0:T(8,128)(2,1)S(1)}, u32[]{:S(2)}, u32[]{:S(2)}) collective-permute-start(bf16[48,768]{1,0:T(8,128)(2,1)S(1)} %dynamic-slice_bitcast_fusion.14), channel_id=1, source_target_pairs={{0,8},{4,12},{8,0},{12,4},{16,24},{20,28},{24,16},{28,20},{1,9},{5... | collective-permute-start | bytes 221192 | tf_op jit(solution)/shard_map/ppermute | solution.py:27
  225.6 4.0 %collective-permute-start.13 = (f32[1,9216]{1,0:T(1,128)S(1)}, f32[1,9216]{1,0:T(1,128)S(1)}, u32[]{:S(2)}, u32[]{:S(2)}) collective-permute-start(f32[1,9216]{1,0:T(1,128)S(1)} %add.380), channel_id=1, source_target_pairs={{0,8},{4,12},{8,0},{12,4},{16,24},{20,28},{24,16},{28,20},{1,9},{5... | collective-permute-start | bytes 110600 | tf_op jit(solution)/shard_map/ppermute | solution.py:27
  226.2 6.2 %collective-permute-start.27 = (bf16[24,768]{1,0:T(8,128)(2,1)S(1)}, bf16[24,768]{1,0:T(8,128)(2,1)S(1)}, u32[]{:S(2)}, u32[]{:S(2)}) collective-permute-start(bf16[24,768]{1,0:T(8,128)(2,1)S(1)} %dynamic-slice_bitcast_fusion.15), channel_id=1, source_target_pairs={{0,16},{4,20},{8,24},{12,28},{16,0},{20,4},{24,8},{28,12},{1,17},{... | collective-permute-start | bytes 110600 | tf_op jit(solution)/shard_map/ppermute | solution.py:27
  228.8 5.1 %copy-start.4 = (bf16[768,2304]{1,0:T(8,128)(2,1)S(1)}, bf16[768,2304]{1,0:T(8,128)(2,1)}, u32[]{:S(2)}) copy-start(bf16[768,2304]{1,0:T(8,128)(2,1)} %copy-done.3) | copy-start | bytes 10616836
  229.0 58.2 %collective-permute-start.39 = (bf16[2,768,768]{2,1,0:T(8,128)(2,1)S(1)}, bf16[2,768,768]{2,1,0:T(8,128)(2,1)S(1)}, u32[]{:S(2)}, u32[]{:S(2)}) collective-permute-start(bf16[2,768,768]{2,1,0:T(8,128)(2,1)S(1)} %dynamic-slice_bitcast_fusion), channel_id=1, source_target_pairs={{0,1},{1,0},{2,3},{3,2},{4,5},{5,4},{6,7},{7,6},{8,9},{9,8},{10,11... | collective-permute-start | bytes 7077896 | tf_op jit(solution)/shard_map/ppermute | solution.py:27
  229.7 15.5 %collective-permute-start.14 = (f32[1,9216]{1,0:T(1,128)S(1)}, f32[1,9216]{1,0:T(1,128)S(1)}, u32[]{:S(2)}, u32[]{:S(2)}) collective-permute-start(f32[1,9216]{1,0:T(1,128)S(1)} %add.381), channel_id=1, source_target_pairs={{0,16},{4,20},{8,24},{12,28},{16,0},{20,4},{24,8},{28,12},{1,17},{... | collective-permute-start | bytes 110600 | tf_op jit(solution)/shard_map/ppermute | solution.py:27
  232.4 4.2 %copy-start.26 = (f32[768]{0:T(1024)S(1)}, f32[768]{0:T(1024)}, u32[]{:S(2)}) copy-start(f32[768]{0:T(1024)} %reshape.321) | copy-start | bytes 9220
  232.4 4.2 %copy-start.27 = (f32[768]{0:T(1024)S(1)}, f32[768]{0:T(1024)}, u32[]{:S(2)}) copy-start(f32[768]{0:T(1024)} %reshape.317) | copy-start | bytes 9220
  232.4 4.1 %copy-start.29 = (f32[1024,768]{1,0:T(8,128)S(1)}, f32[1024,768]{1,0:T(8,128)}, u32[]{:S(2)}) copy-start(f32[1024,768]{1,0:T(8,128)} %fusion.103) | copy-start | bytes 9437188
  232.4 12.8 %collective-permute-start.28 = (bf16[24,768]{1,0:T(8,128)(2,1)S(1)}, bf16[24,768]{1,0:T(8,128)(2,1)S(1)}, u32[]{:S(2)}, u32[]{:S(2)}) collective-permute-start(bf16[24,768]{1,0:T(8,128)(2,1)S(1)} %fusion.96), channel_id=1, source_target_pairs={{0,16},{4,20},{8,24},{12,28},{16,0},{20,4},{24,8},{28,12},{1,17},{... | collective-permute-start | bytes 110600 | tf_op jit(solution)/shard_map/ppermute | solution.py:27
  236.0 19.8 %collective-permute-start.16 = (bf16[1,192,2304]{2,1,0:T(8,128)(2,1)S(1)}, bf16[1,192,2304]{2,1,0:T(8,128)(2,1)S(1)}, u32[]{:S(2)}, u32[]{:S(2)}) collective-permute-start(bf16[1,192,2304]{2,1,0:T(8,128)(2,1)S(1)} %constant_dynamic-slice_fusion.8), channel_id=1, source_target_pairs={{0,2},{1,3},{2,0},{3,1},{4,6},{5,7},{6,4},{7,5},{8,10},{9,11},{10,... | collective-permute-start | bytes 2654216 | tf_op jit(solution)/shard_map/ppermute | solution.py:27
  245.3 13.9 %collective-permute-start.29 = (bf16[48,768]{1,0:T(8,128)(2,1)S(1)}, bf16[48,768]{1,0:T(8,128)(2,1)S(1)}, u32[]{:S(2)}, u32[]{:S(2)}) collective-permute-start(bf16[48,768]{1,0:T(8,128)(2,1)S(1)} %pad_maximum_fusion.11), channel_id=1, source_target_pairs={{0,8},{4,12},{8,0},{12,4},{16,24},{20,28},{24,16},{28,20},{1,9},{5... | collective-permute-start | bytes 221192 | tf_op jit(solution)/shard_map/ppermute | solution.py:27
  256.1 11.0 %collective-permute-start.17 = (bf16[96,2304]{1,0:T(8,128)(2,1)S(1)}, bf16[96,2304]{1,0:T(8,128)(2,1)S(1)}, u32[]{:S(2)}, u32[]{:S(2)}) collective-permute-start(bf16[96,2304]{1,0:T(8,128)(2,1)S(1)} %dynamic-slice_bitcast_fusion.6), channel_id=1, source_target_pairs={{0,4},{4,0},{8,12},{12,8},{16,20},{20,16},{24,28},{28,24},{1,5},{5... | collective-permute-start | bytes 1327112 | tf_op jit(solution)/shard_map/ppermute | solution.py:27
  257.8 134.0 %copy-start.25 = (f32[1,192]{1,0:T(1,128)}, f32[1,192]{1,0:T(1,128)S(1)}, u32[]{:S(2)}) copy-start(f32[1,192]{1,0:T(1,128)S(1)} %get-tuple-element.78) | copy-start | bytes 2308
  259.2 9.5 %collective-permute-start.30 = (bf16[96,768]{1,0:T(8,128)(2,1)S(1)}, bf16[96,768]{1,0:T(8,128)(2,1)S(1)}, u32[]{:S(2)}, u32[]{:S(2)}) collective-permute-start(bf16[96,768]{1,0:T(8,128)(2,1)S(1)} %pad_maximum_fusion.10), channel_id=1, source_target_pairs={{0,4},{4,0},{8,12},{12,8},{16,20},{20,16},{24,28},{28,24},{1,5},{5... | collective-permute-start | bytes 442376 | tf_op jit(solution)/shard_map/ppermute | solution.py:27
  267.2 7.2 %collective-permute-start.18 = (bf16[48,2304]{1,0:T(8,128)(2,1)S(1)}, bf16[48,2304]{1,0:T(8,128)(2,1)S(1)}, u32[]{:S(2)}, u32[]{:S(2)}) collective-permute-start(bf16[48,2304]{1,0:T(8,128)(2,1)S(1)} %dynamic-slice_bitcast_fusion.9), channel_id=1, source_target_pairs={{0,8},{4,12},{8,0},{12,4},{16,24},{20,28},{24,16},{28,20},{1,9},{5... | collective-permute-start | bytes 663560 | tf_op jit(solution)/shard_map/ppermute | solution.py:27
  274.5 6.6 %collective-permute-start.19 = (bf16[24,2304]{1,0:T(8,128)(2,1)S(1)}, bf16[24,2304]{1,0:T(8,128)(2,1)S(1)}, u32[]{:S(2)}, u32[]{:S(2)}) collective-permute-start(bf16[24,2304]{1,0:T(8,128)(2,1)S(1)} %dynamic-slice_bitcast_fusion.13), channel_id=1, source_target_pairs={{0,16},{4,20},{8,24},{12,28},{16,0},{20,4},{24,8},{28,12},{1,17},{... | collective-permute-start | bytes 331784 | tf_op jit(solution)/shard_map/ppermute | solution.py:27
  281.1 6.0 %collective-permute-start.20 = (bf16[24,2304]{1,0:T(8,128)(2,1)S(1)}, bf16[24,2304]{1,0:T(8,128)(2,1)S(1)}, u32[]{:S(2)}, u32[]{:S(2)}) collective-permute-start(bf16[24,2304]{1,0:T(8,128)(2,1)S(1)} %fusion.94), channel_id=1, source_target_pairs={{0,16},{4,20},{8,24},{12,28},{16,0},{20,4},{24,8},{28,12},{1,17},{... | collective-permute-start | bytes 331784 | tf_op jit(solution)/shard_map/ppermute | solution.py:27
  281.3 29.0 %collective-permute-start.32 = (bf16[1,192,3072]{2,1,0:T(8,128)(2,1)S(1)}, bf16[1,192,3072]{2,1,0:T(8,128)(2,1)S(1)}, u32[]{:S(2)}, u32[]{:S(2)}) collective-permute-start(bf16[1,192,3072]{2,1,0:T(8,128)(2,1)S(1)} %constant_dynamic-slice_fusion.2), channel_id=1, source_target_pairs={{0,2},{1,3},{2,0},{3,1},{4,6},{5,7},{6,4},{7,5},{8,10},{9,11},{10,... | collective-permute-start | bytes 3538952 | tf_op jit(solution)/shard_map/ppermute | solution.py:27
  287.1 6.0 %collective-permute-start.21 = (bf16[48,2304]{1,0:T(8,128)(2,1)S(1)}, bf16[48,2304]{1,0:T(8,128)(2,1)S(1)}, u32[]{:S(2)}, u32[]{:S(2)}) collective-permute-start(bf16[48,2304]{1,0:T(8,128)(2,1)S(1)} %pad_maximum_fusion.9), channel_id=1, source_target_pairs={{0,8},{4,12},{8,0},{12,4},{16,24},{20,28},{24,16},{28,20},{1,9},{5... | collective-permute-start | bytes 663560 | tf_op jit(solution)/shard_map/ppermute | solution.py:27
  287.9 38.5 %collective-permute-start.40 = (bf16[1,768,768]{2,1,0:T(8,128)(2,1)S(1)}, bf16[1,768,768]{2,1,0:T(8,128)(2,1)S(1)}, u32[]{:S(2)}, u32[]{:S(2)}) collective-permute-start(bf16[1,768,768]{2,1,0:T(8,128)(2,1)S(1)} %constant_dynamic-slice_fusion), channel_id=1, source_target_pairs={{0,2},{1,3},{2,0},{3,1},{4,6},{5,7},{6,4},{7,5},{8,10},{9,11},{10,... | collective-permute-start | bytes 3538952 | tf_op jit(solution)/shard_map/ppermute | solution.py:27
  293.2 18.5 %collective-permute-start.22 = (bf16[96,2304]{1,0:T(8,128)(2,1)S(1)}, bf16[96,2304]{1,0:T(8,128)(2,1)S(1)}, u32[]{:S(2)}, u32[]{:S(2)}) collective-permute-start(bf16[96,2304]{1,0:T(8,128)(2,1)S(1)} %pad_maximum_fusion.6), channel_id=1, source_target_pairs={{0,4},{4,0},{8,12},{12,8},{16,20},{20,16},{24,28},{28,24},{1,5},{5... | collective-permute-start | bytes 1327112 | tf_op jit(solution)/shard_map/ppermute | solution.py:27
  310.7 17.2 %collective-permute-start.33 = (bf16[96,3072]{1,0:T(8,128)(2,1)S(1)}, bf16[96,3072]{1,0:T(8,128)(2,1)S(1)}, u32[]{:S(2)}, u32[]{:S(2)}) collective-permute-start(bf16[96,3072]{1,0:T(8,128)(2,1)S(1)} %dynamic-slice_bitcast_fusion.4), channel_id=1, source_target_pairs={{0,4},{4,0},{8,12},{12,8},{16,20},{20,16},{24,28},{28,24},{1,5},{5... | collective-permute-start | bytes 1769480 | tf_op jit(solution)/shard_map/ppermute | solution.py:27
  326.7 9.9 %collective-permute-start.41 = (bf16[384,768]{1,0:T(8,128)(2,1)S(1)}, bf16[384,768]{1,0:T(8,128)(2,1)S(1)}, u32[]{:S(2)}, u32[]{:S(2)}) collective-permute-start(bf16[384,768]{1,0:T(8,128)(2,1)S(1)} %dynamic-slice_bitcast_fusion.3), channel_id=1, source_target_pairs={{0,4},{4,0},{8,12},{12,8},{16,20},{20,16},{24,28},{28,24},{1,5},{5... | collective-permute-start | bytes 1769480 | tf_op jit(solution)/shard_map/ppermute | solution.py:27
  328.1 9.6 %collective-permute-start.34 = (bf16[48,3072]{1,0:T(8,128)(2,1)S(1)}, bf16[48,3072]{1,0:T(8,128)(2,1)S(1)}, u32[]{:S(2)}, u32[]{:S(2)}) collective-permute-start(bf16[48,3072]{1,0:T(8,128)(2,1)S(1)} %dynamic-slice_bitcast_fusion.8), channel_id=1, source_target_pairs={{0,8},{4,12},{8,0},{12,4},{16,24},{20,28},{24,16},{28,20},{1,9},{5... | collective-permute-start | bytes 884744 | tf_op jit(solution)/shard_map/ppermute | solution.py:27
  336.9 9.7 %collective-permute-start.42 = (bf16[192,768]{1,0:T(8,128)(2,1)S(1)}, bf16[192,768]{1,0:T(8,128)(2,1)S(1)}, u32[]{:S(2)}, u32[]{:S(2)}) collective-permute-start(bf16[192,768]{1,0:T(8,128)(2,1)S(1)} %dynamic-slice_bitcast_fusion.7), channel_id=1, source_target_pairs={{0,8},{4,12},{8,0},{12,4},{16,24},{20,28},{24,16},{28,20},{1,9},{5... | collective-permute-start | bytes 884744 | tf_op jit(solution)/shard_map/ppermute | solution.py:27
  337.7 10.7 %collective-permute-start.35 = (bf16[24,3072]{1,0:T(8,128)(2,1)S(1)}, bf16[24,3072]{1,0:T(8,128)(2,1)S(1)}, u32[]{:S(2)}, u32[]{:S(2)}) collective-permute-start(bf16[24,3072]{1,0:T(8,128)(2,1)S(1)} %dynamic-slice_bitcast_fusion.11), channel_id=1, source_target_pairs={{0,16},{4,20},{8,24},{12,28},{16,0},{20,4},{24,8},{28,12},{1,17},{... | collective-permute-start | bytes 442376 | tf_op jit(solution)/shard_map/ppermute | solution.py:27
  346.7 9.0 %collective-permute-start.43 = (bf16[96,768]{1,0:T(8,128)(2,1)S(1)}, bf16[96,768]{1,0:T(8,128)(2,1)S(1)}, u32[]{:S(2)}, u32[]{:S(2)}) collective-permute-start(bf16[96,768]{1,0:T(8,128)(2,1)S(1)} %dynamic-slice_bitcast_fusion.10), channel_id=1, source_target_pairs={{0,16},{4,20},{8,24},{12,28},{16,0},{20,4},{24,8},{28,12},{1,17},{... | collective-permute-start | bytes 442376 | tf_op jit(solution)/shard_map/ppermute | solution.py:27
  348.5 10.4 %collective-permute-start.36 = (bf16[24,3072]{1,0:T(8,128)(2,1)S(1)}, bf16[24,3072]{1,0:T(8,128)(2,1)S(1)}, u32[]{:S(2)}, u32[]{:S(2)}) collective-permute-start(bf16[24,3072]{1,0:T(8,128)(2,1)S(1)} %fusion.92), channel_id=1, source_target_pairs={{0,16},{4,20},{8,24},{12,28},{16,0},{20,4},{24,8},{28,12},{1,17},{... | collective-permute-start | bytes 442376 | tf_op jit(solution)/shard_map/ppermute | solution.py:27
  355.7 6.2 %collective-permute-start.44 = (bf16[96,768]{1,0:T(8,128)(2,1)S(1)}, bf16[96,768]{1,0:T(8,128)(2,1)S(1)}, u32[]{:S(2)}, u32[]{:S(2)}) collective-permute-start(bf16[96,768]{1,0:T(8,128)(2,1)S(1)} %fusion.91), channel_id=1, source_target_pairs={{0,16},{4,20},{8,24},{12,28},{16,0},{20,4},{24,8},{28,12},{1,17},{... | collective-permute-start | bytes 442376 | tf_op jit(solution)/shard_map/ppermute | solution.py:27
  358.9 9.3 %collective-permute-start.37 = (bf16[48,3072]{1,0:T(8,128)(2,1)S(1)}, bf16[48,3072]{1,0:T(8,128)(2,1)S(1)}, u32[]{:S(2)}, u32[]{:S(2)}) collective-permute-start(bf16[48,3072]{1,0:T(8,128)(2,1)S(1)} %pad_maximum_fusion.7), channel_id=1, source_target_pairs={{0,8},{4,12},{8,0},{12,4},{16,24},{20,28},{24,16},{28,20},{1,9},{5... | collective-permute-start | bytes 884744 | tf_op jit(solution)/shard_map/ppermute | solution.py:27
  362.0 9.4 %collective-permute-start.45 = (bf16[192,768]{1,0:T(8,128)(2,1)S(1)}, bf16[192,768]{1,0:T(8,128)(2,1)S(1)}, u32[]{:S(2)}, u32[]{:S(2)}) collective-permute-start(bf16[192,768]{1,0:T(8,128)(2,1)S(1)} %pad_maximum_fusion.8), channel_id=1, source_target_pairs={{0,8},{4,12},{8,0},{12,4},{16,24},{20,28},{24,16},{28,20},{1,9},{5... | collective-permute-start | bytes 884744 | tf_op jit(solution)/shard_map/ppermute | solution.py:27
  368.4 15.3 %collective-permute-start.38 = (bf16[96,3072]{1,0:T(8,128)(2,1)S(1)}, bf16[96,3072]{1,0:T(8,128)(2,1)S(1)}, u32[]{:S(2)}, u32[]{:S(2)}) collective-permute-start(bf16[96,3072]{1,0:T(8,128)(2,1)S(1)} %pad_maximum_fusion.4), channel_id=1, source_target_pairs={{0,4},{4,0},{8,12},{12,8},{16,20},{20,16},{24,28},{28,24},{1,5},{5... | collective-permute-start | bytes 1769480 | tf_op jit(solution)/shard_map/ppermute | solution.py:27
  371.5 18.5 %collective-permute-start.46 = (bf16[384,768]{1,0:T(8,128)(2,1)S(1)}, bf16[384,768]{1,0:T(8,128)(2,1)S(1)}, u32[]{:S(2)}, u32[]{:S(2)}) collective-permute-start(bf16[384,768]{1,0:T(8,128)(2,1)S(1)} %pad_maximum_fusion.5), channel_id=1, source_target_pairs={{0,4},{4,0},{8,12},{12,8},{16,20},{20,16},{24,28},{28,24},{1,5},{5... | collective-permute-start | bytes 1769480 | tf_op jit(solution)/shard_map/ppermute | solution.py:27
  (13 other events, 22.3 us)
